TPU v7x, 128 devices: a whole 4x4x4 slice. The times are simulated.
128 devices in a mesh: dp: 4 (over x), ctx: 32 (over z, y, core).
Axes of the slice: x: 4, y: 4, z: 4, core: 2. Of those that a mesh axis runs over, the one named last changes fastest.
Arguments:
- query_act: bfloat16 [4, 4096, 4096], P('dp', 'ctx'), may hold values from -22 to 22
- key_act: bfloat16 [4, 4096, 4096], P('dp', 'ctx'), may hold values from -6 to 6
- value_act: bfloat16 [4, 4096, 4096], P('dp', 'ctx'), may hold values from -6 to 6
- out_grad: bfloat16 [4, 4096, 4096], P('dp', 'ctx'), may hold values from -6 to 6
- filter_weight: float32 [4096, 4096], P('ctx'), may hold values from -36 to 36
- first_moment: float32 [4096, 4096], P('ctx', 'dp'), may hold values from -3 to 3
- second_moment: float32 [4096, 4096], P('ctx', 'dp'), may hold values from 0.05 to 2
Outputs:
- query_grad: bfloat16 [4, 4096, 4096], P('dp', 'ctx')
- key_grad: bfloat16 [4, 4096, 4096], P('dp', 'ctx')
- value_grad: bfloat16 [4, 4096, 4096], P('dp', 'ctx')
- new_filter: float32 [4096, 4096], P('ctx', 'dp')
- new_first: float32 [4096, 4096], P('ctx', 'dp')
- new_second: float32 [4096, 4096], P('ctx', 'dp')
All inputs are finite; a program needn't handle non-finite values.
Results may differ from a plain program's by a relative error of at most 0.002.
Values sent between devices are 32-bit elements; how exact they have to be, the bound alone decides.
A program may use at most 128 MiB of HBM per device.

v0:
```python
import math

import jax
import jax.numpy as jnp
from jax import lax
from jax.sharding import PartitionSpec as P

highest = lax.Precision.HIGHEST
beta_first = 0.9
beta_second = 0.95
learn_rate = 0.01
decay_rate = 0.1
adam_epsilon = 1e-08
correct_first = 0.9999734386011124
correct_second = 0.994079470779666


def counting(amount):
    return jnp.arange(amount, dtype=jnp.int32)


def angle_table(outer_ids, inner_ids, period, direction):
    product = outer_ids[:, None] * inner_ids[None, :] % period
    angles = direction * 2.0 * math.pi / period * product.astype(jnp.float32)
    return (jnp.cos(angles), jnp.sin(angles))


def lead_forward(values, part_count):
    cosine_table, sine_table = angle_table(
        counting(2 * part_count), counting(part_count), 2 * part_count, -1.0
    )
    table = jnp.stack([cosine_table, sine_table])
    return jnp.einsum("rka,ajc->rkjc", table, values, precision=highest)


def lead_inverse(stacked, part_count, period):
    cosine_table, sine_table = angle_table(
        counting(part_count), counting(2 * part_count), 2 * part_count, 1.0
    )
    table = jnp.stack([cosine_table, -sine_table])
    return jnp.einsum("qka,qajc->kjc", table, stacked, precision=highest) * (1.0 / period)


def middle_section(stacked, direction):
    span_length = stacked.shape[2]
    cosine_table, sine_table = angle_table(
        counting(span_length), counting(span_length), span_length, direction
    )
    table = jnp.stack(
        [jnp.stack([cosine_table, -sine_table]), jnp.stack([sine_table, cosine_table])]
    )
    return jnp.einsum("rqmj,qkjc->rkmc", table, stacked, precision=highest)


def rotate(stacked, row_ids, col_ids, period, direction):
    cosine_table, sine_table = angle_table(row_ids, col_ids, period, direction)
    cosine_table = cosine_table[:, :, None]
    sine_table = sine_table[:, :, None]
    real_part = stacked[0]
    imaginary = stacked[1]
    return jnp.stack(
        [
            real_part * cosine_table - imaginary * sine_table,
            real_part * sine_table + imaginary * cosine_table,
        ]
    )


def spectral_products(kernel_spec, mixed_spec, gated_spec):
    kernel_real, kernel_imaginary = (kernel_spec[0], kernel_spec[1])
    mixed_real, mixed_imaginary = (mixed_spec[0], mixed_spec[1])
    gated_real, gated_imaginary = (gated_spec[0], gated_spec[1])
    forward_product = jnp.stack(
        [
            kernel_real * mixed_real - kernel_imaginary * mixed_imaginary,
            kernel_real * mixed_imaginary + kernel_imaginary * mixed_real,
        ]
    )
    backward_product = jnp.stack(
        [
            kernel_real * gated_real + kernel_imaginary * gated_imaginary,
            kernel_real * gated_imaginary - kernel_imaginary * gated_real,
        ]
    )
    lag_product = jnp.stack(
        [
            mixed_real * gated_real + mixed_imaginary * gated_imaginary,
            mixed_real * gated_imaginary - mixed_imaginary * gated_real,
        ]
    )
    return (forward_product, backward_product, lag_product)


def channel_work(members):
    part_count = lax.axis_size("ctx")
    total_rows = members[0].shape[0]
    trailing = tuple(members[0].shape[1:])
    span_length = total_rows // part_count
    period = 2 * total_rows
    row_ids = counting(2 * part_count)
    col_ids = counting(span_length)
    spectra = []
    for member in members:
        shaped = member.reshape(part_count, span_length, -1)
        stacked = lead_forward(shaped, part_count)
        stacked = rotate(stacked, row_ids, col_ids, period, -1.0)
        spectra.append(middle_section(stacked, -1.0))
    products = spectral_products(spectra[1], spectra[0], spectra[2])
    results = []
    for product in products:
        stacked = middle_section(product, 1.0)
        stacked = rotate(stacked, row_ids, col_ids, period, 1.0)
        results.append(lead_inverse(stacked, part_count, period).reshape((total_rows,) + trailing))
    return (results[0], results[1], results[2])


def group_order(values, data_count, part_count, sub_width):
    length_dev = values.shape[0]
    shaped = values.reshape(length_dev, data_count, part_count, sub_width)
    return jnp.transpose(shaped, (0, 2, 1, 3)).reshape(
        length_dev, part_count, data_count * sub_width
    )


def plain_order(values, data_count, part_count, sub_width):
    length_dev = values.shape[0]
    shaped = values.reshape(length_dev, part_count, data_count, sub_width)
    return jnp.transpose(shaped, (0, 2, 1, 3)).reshape(
        length_dev, data_count * part_count * sub_width
    )


def on_device(query_act, key_act, value_act, out_grad, filter_weight, first_moment, second_moment):
    keys_float = key_act[0].astype(jnp.float32)
    values_float = value_act[0].astype(jnp.float32)
    upstream = out_grad[0].astype(jnp.float32)
    mixed_in = keys_float * values_float
    gated_in = upstream * query_act[0].astype(jnp.float32)
    part_count = lax.axis_size("ctx")
    data_count = lax.axis_size("dp")
    length_dev = mixed_in.shape[0]
    channel_count = filter_weight.shape[1]
    sub_width = channel_count // (data_count * part_count)
    kernel = filter_weight * (part_count * length_dev) ** (-0.5)
    arrived = channel_work(
        (
            lax.all_to_all(
                group_order(mixed_in, data_count, part_count, sub_width),
                "ctx",
                split_axis=1,
                concat_axis=0,
                tiled=True,
            ),
            lax.all_to_all(
                group_order(kernel, data_count, part_count, sub_width),
                "ctx",
                split_axis=1,
                concat_axis=0,
                tiled=True,
            ),
            lax.all_to_all(
                group_order(gated_in, data_count, part_count, sub_width),
                "ctx",
                split_axis=1,
                concat_axis=0,
                tiled=True,
            ),
        )
    )
    returned = (
        lax.all_to_all(arrived[0], "ctx", split_axis=0, concat_axis=1, tiled=True),
        lax.all_to_all(arrived[1], "ctx", split_axis=0, concat_axis=1, tiled=True),
        lax.all_to_all(arrived[2], "ctx", split_axis=0, concat_axis=1, tiled=True),
    )
    conv_out = plain_order(returned[0], data_count, part_count, sub_width)
    back_in = plain_order(returned[1], data_count, part_count, sub_width)
    lag_grad = plain_order(returned[2], data_count, part_count, sub_width)
    summed = lax.psum_scatter(lag_grad, "dp", scatter_dimension=1, tiled=True)
    query_grad = (upstream * conv_out).astype(jnp.bfloat16)[None]
    key_grad = (back_in * values_float).astype(jnp.bfloat16)[None]
    value_grad = (back_in * keys_float).astype(jnp.bfloat16)[None]
    local_square = jnp.sum(summed * summed)
    local_bad = jnp.sum(jnp.logical_not(jnp.isfinite(summed)).astype(jnp.float32))
    total_sq, bad_count = lax.psum((local_square, local_bad), ("dp", "ctx"))
    shard_width = summed.shape[1]
    own_filter = lax.dynamic_slice_in_dim(
        filter_weight, lax.axis_index("dp") * shard_width, shard_width, 1
    )
    root_mean = jnp.sqrt(total_sq / float(part_count * length_dev * channel_count) + 1e-06)
    clipped = summed * jnp.minimum(1.0, 1.0 / root_mean)
    first_next = beta_first * first_moment + (1.0 - beta_first) * clipped
    second_next = beta_second * second_moment + (1.0 - beta_second) * clipped * clipped
    update = (
        first_next / correct_first / (jnp.sqrt(second_next / correct_second) + adam_epsilon)
        + decay_rate * own_filter
    )
    filter_next = own_filter - learn_rate * update
    commit = bad_count == 0.0
    return (
        query_grad,
        key_grad,
        value_grad,
        jnp.where(commit, filter_next, own_filter),
        jnp.where(commit, first_next, first_moment),
        jnp.where(commit, second_next, second_moment),
    )


def solution(mesh):
    return jax.shard_map(
        on_device,
        mesh=mesh,
        in_specs=(
            P("dp", "ctx", None),
            P("dp", "ctx", None),
            P("dp", "ctx", None),
            P("dp", "ctx", None),
            P("ctx", None),
            P("ctx", "dp"),
            P("ctx", "dp"),
        ),
        out_specs=(
            P("dp", "ctx", None),
            P("dp", "ctx", None),
            P("dp", "ctx", None),
            P("ctx", "dp"),
            P("ctx", "dp"),
            P("ctx", "dp"),
        ),
        check_vma=False,
    )
```

profile of v0, /device:TPU:1, one launch (start us, length us, event | category | flops | bytes accessed | tf_op | source)
XLA Modules:
  0.0 528.1 jit_solution(15471047882564085629)
XLA Ops:
  7.2 1.9 copy.151
  11.1 2.9 copy.153
  14.0 9.6 %all-to-all-start = ((f32[128,32,128]{2,0,1:T(8,128)}), f32[128,32,128]{2,0,1:T(8,128)S(1)}, u32[]{:S(2)}, u32[]{:S(2)}) async-start(f32[128,32,128]{2,0,1:T(8,128)} %copy.153), calls=%async_computation | async-start | bytes 4194304 | tf_op jit(solution)/shard_map/all_to_all | solution.py:154
  25.3 2.6 copy.169
  30.9 2.9 copy.171
  33.8 17.7 %all-to-all-done = f32[128,32,128]{2,0,1:T(8,128)S(1)} async-done(((f32[128,32,128]{2,0,1:T(8,128)}), f32[128,32,128]{2,0,1:T(8,128)S(1)}, u32[]{:S(2)}, u32[]{:S(2)}) %all-to-all-start) | async-done | bytes 2097184 | tf_op jit(solution)/shard_map/all_to_all | solution.py:154
  51.5 6.7 %all-to-all-start.3 = ((f32[128,32,128]{2,0,1:T(8,128)}), f32[128,32,128]{2,0,1:T(8,128)}, u32[]{:S(2)}, u32[]{:S(2)}) async-start(f32[128,32,128]{2,0,1:T(8,128)} %copy.171), calls=%async_computation.3 | async-start | bytes 4194304 | tf_op jit(solution)/shard_map/all_to_all | solution.py:161
  63.3 10.4 %fusion.34 = f32[2,64,128,128]{3,1,2,0:T(8,128)} fusion(f32[128,32,128]{2,0,1:T(8,128)S(1)} %all-to-all-done, f32[1,64,32]{1,2,0:T(8,128)S(1)} %get-tuple-element.68, f32[1,64,32]{1,2,0:T(8,128)S(1)} %get-tuple-element.69), kind=kOutput, calls=%fused_computation.60 | convolution fusion | flops 805310464 | bytes 10502144 | tf_op jit(solution)/shard_map/rka,ajc->rkjc/dot_general | solution.py:33
  73.8 12.4 %all-to-all-done.3 = f32[128,32,128]{2,0,1:T(8,128)} async-done(((f32[128,32,128]{2,0,1:T(8,128)}), f32[128,32,128]{2,0,1:T(8,128)}, u32[]{:S(2)}, u32[]{:S(2)}) %all-to-all-start.3) | async-done | bytes 2097184 | tf_op jit(solution)/shard_map/all_to_all | solution.py:161
  86.2 8.9 %fusion.30 = f32[2,64,128,128]{3,1,2,0:T(8,128)S(1)} fusion(f32[128,32,128]{2,0,1:T(8,128)} %all-to-all-done.3, f32[1,64,32]{1,2,0:T(8,128)S(1)} %get-tuple-element.68, f32[1,64,32]{1,2,0:T(8,128)S(1)} %get-tuple-element.69), kind=kOutput, calls=%fused_computation.56 | convolution fusion | flops 805310464 | bytes 10502144 | tf_op jit(solution)/shard_map/rka,ajc->rkjc/dot_general | solution.py:33
  95.2 6.7 %multiply_subtract_fusion.4 = (f32[1,64,128,128]{3,1,2,0:T(8,128)S(1)}, f32[1,64,128,128]{3,1,2,0:T(8,128)}, f32[1,64,128,128]{3,1,2,0:T(8,128)S(1)}, f32[1,64,128,128]{3,1,2,0:T(8,128)}) fusion(f32[2,64,128,128]{3,1,2,0:T(8,128)S(1)} %fusion.30, f32[64,128]{0,1:T(8,128)S(1)} %copy-done.15, f32[64,128]{0,1:T(8,128)S(1)} %copy-done.13, ...), kind=kLoop, calls=%fused_computation.33 | loop fusion | flops 12582912 | bytes 33619968 | tf_op jit(solution)/shard_map/sub | solution.py:63
  101.9 3.2 maximum_bitcast_fusion
  105.1 3.5 maximum_bitcast_fusion.4
  108.5 17.8 %fusion.15 = f32[2,64,128,128]{2,3,0,1:T(8,128)S(1)} fusion(f32[2,64,128,128,1]{3,1,2,0,4:T(8,128)S(1)} %maximum_bitcast_fusion, f32[1,2,128,128]{3,2,1,0:T(8,128)S(1)} %copy-done.9, f32[1,2,128,128]{3,2,1,0:T(8,128)S(1)} %get-tuple-element.66), kind=kOutput, calls=%fused_computation.42 | convolution fusion | flops 6442516480 | bytes 17039360 | tf_op jit(solution)/shard_map/rqmj,qkjc->rkmc/dot_general | solution.py:52
  126.4 18.3 %fusion.21 = f32[2,64,128,128]{2,3,0,1:T(8,128)S(1)} fusion(f32[2,64,128,128,1]{3,1,2,0,4:T(8,128)S(1)} %maximum_bitcast_fusion.4, f32[1,2,128,128]{3,2,1,0:T(8,128)S(1)} %copy-done.9, f32[1,2,128,128]{3,2,1,0:T(8,128)S(1)} %get-tuple-element.66), kind=kOutput, calls=%fused_computation.44 | convolution fusion | flops 6442516480 | bytes 17039360 | tf_op jit(solution)/shard_map/rqmj,qkjc->rkmc/dot_general | solution.py:52
  148.0 8.0 %fusion.25 = f32[2,64,128,128]{2,3,0,1:T(8,128)S(1)} fusion(f32[1,64,128,128]{2,3,0,1:T(8,128)S(1)} %get-tuple-element.37, f32[1,64,128,128]{2,3,0,1:T(8,128)S(1)} %get-tuple-element.36, f32[1,2,128,128]{3,2,1,0:T(8,128)S(1)} %get-tuple-element.65, f32[1,2,128,128]{3,2,1,0:T(8,128)S(1)} %get-tuple-element.64), kind=kOutput, calls=%fused_computation.46 | convolution fusion | flops 6444613632 | bytes 17039360 | tf_op jit(solution)/shard_map/rqmj,qkjc->rkmc/dot_general | solution.py:52
  156.0 2.0 multiply_subtract_fusion.2
  158.0 3.9 pad_maximum_fusion.1
  161.8 8.8 %copy.174 = f32[2,64,128,128]{3,1,0,2:T(8,128)} copy(f32[2,64,128,128]{2,3,0,1:T(8,128)} %pad_maximum_fusion.1) | data formatting | bytes 16777216 | tf_op jit(solution)/shard_map/stack | solution.py:61
  170.7 6.7 %bitcast_multiply_fusion.1 = f32[32,128,128]{2,0,1:T(8,128)S(1)} fusion(f32[2,64,128,128]{3,1,0,2:T(8,128)} %copy.174, f32[1,32,64]{2,1,0:T(8,128)S(1)} %get-tuple-element.76, f32[1,32,64]{2,1,0:T(8,128)S(1)} %copy-done.21), kind=kOutput, calls=%fused_computation.63 | convolution fusion | flops 805834752 | bytes 10502144 | tf_op jit(solution)/shard_map/qka,qajc->kjc/dot_general | solution.py:41
  177.3 2.6 copy.175
  179.9 6.1 %all-to-all-start.4 = ((f32[4096,1,128]{2,1,0:T(1,128)}), f32[4096,1,128]{2,1,0:T(1,128)S(1)}, u32[]{:S(2)}, u32[]{:S(2)}) async-start(f32[4096,1,128]{2,1,0:T(1,128)} %bitcast.174), calls=%async_computation.4 | async-start | bytes 4194304 | tf_op jit(solution)/shard_map/all_to_all | solution.py:172
  187.8 2.3 copy.159
  190.1 23.8 %all-to-all-done.4 = f32[4096,1,128]{2,1,0:T(1,128)S(1)} async-done(((f32[4096,1,128]{2,1,0:T(1,128)}), f32[4096,1,128]{2,1,0:T(1,128)S(1)}, u32[]{:S(2)}, u32[]{:S(2)}) %all-to-all-start.4) | async-done | bytes 2097184 | tf_op jit(solution)/shard_map/all_to_all | solution.py:172
  221.6 34.5 %all_to_all.90 = f32[128,32,128]{2,0,1:T(8,128)S(1)} all-to-all(f32[128,32,128]{2,0,1:T(8,128)} %copy.161), channel_id=1, replica_groups=mesh['dp'=4,'ctx'=32] {'ctx'}, dimensions={1} | all-to-all | bytes 4194304 | tf_op jit(solution)/shard_map/all_to_all | solution.py:147
  256.1 7.2 %fusion.32 = f32[2,64,128,128]{3,1,2,0:T(8,128)S(1)} fusion(f32[128,32,128]{2,0,1:T(8,128)S(1)} %all_to_all.90, f32[1,64,32]{1,2,0:T(8,128)S(1)} %copy-done.24, f32[1,64,32]{1,2,0:T(8,128)S(1)} %copy-done.26), kind=kOutput, calls=%fused_computation.58 | convolution fusion | flops 805310464 | bytes 10502144 | tf_op jit(solution)/shard_map/rka,ajc->rkjc/dot_general | solution.py:33
  263.4 2.8 multiply_subtract_fusion.7
  266.2 4.2 maximum_bitcast_fusion.1
  270.4 19.5 %fusion.18 = f32[2,64,128,128]{2,3,0,1:T(8,128)} fusion(f32[2,64,128,128,1]{3,1,2,0,4:T(8,128)} %maximum_bitcast_fusion.1, f32[1,2,128,128]{3,2,1,0:T(8,128)S(1)} %copy-done.10, f32[1,2,128,128]{3,2,1,0:T(8,128)S(1)} %get-tuple-element.66), kind=kOutput, calls=%fused_computation.43 | convolution fusion | flops 6442516480 | bytes 17039360 | tf_op jit(solution)/shard_map/rqmj,qkjc->rkmc/dot_general | solution.py:52
  289.9 11.1 %multiply_add_fusion.1 = (f32[1,64,128,128]{2,3,0,1:T(8,128)S(1)}, f32[1,64,128,128]{2,3,0,1:T(8,128)}, f32[1,64,128,128]{2,3,0,1:T(8,128)}, f32[1,64,128,128]{2,3,0,1:T(8,128)}) fusion(f32[2,64,128,128]{2,3,0,1:T(8,128)} %copy-done.1, f32[2,64,128,128]{2,3,0,1:T(8,128)} %fusion.18, f32[2,64,128,128]{2,3,0,1:T(8,128)S(1)} %bitcast.169), kind=kLoop, calls=%fused_computation.27 | loop fusion | flops 12582912 | bytes 41943040 | tf_op jit(solution)/shard_map/add | solution.py:87
  301.0 9.4 %fusion.26 = f32[2,64,128,128]{2,3,0,1:T(8,128)S(1)} fusion(f32[1,64,128,128]{2,3,0,1:T(8,128)} %get-tuple-element.52, f32[1,64,128,128]{2,3,0,1:T(8,128)} %get-tuple-element.53, f32[1,2,128,128]{3,2,1,0:T(8,128)S(1)} %get-tuple-element.65, f32[1,2,128,128]{3,2,1,0:T(8,128)S(1)} %get-tuple-element.64), kind=kOutput, calls=%fused_computation.47 | convolution fusion | flops 6444613632 | bytes 17039360 | tf_op jit(solution)/shard_map/rqmj,qkjc->rkmc/dot_general | solution.py:52
  310.4 8.1 %fusion.24 = f32[2,64,128,128]{2,3,0,1:T(8,128)S(1)} fusion(f32[1,64,128,128]{2,3,0,1:T(8,128)S(1)} %copy-done.3, f32[1,64,128,128]{2,3,0,1:T(8,128)S(1)} %get-tuple-element.34, f32[1,2,128,128]{3,2,1,0:T(8,128)S(1)} %get-tuple-element.65, f32[1,2,128,128]{3,2,1,0:T(8,128)S(1)} %get-tuple-element.64), kind=kOutput, calls=%fused_computation.45 | convolution fusion | flops 6444613632 | bytes 17039360 | tf_op jit(solution)/shard_map/rqmj,qkjc->rkmc/dot_general | solution.py:52
  318.5 6.1 %multiply_subtract_fusion = (f32[1,64,128,128]{2,3,0,1:T(8,128)S(1)}, f32[1,64,128,128]{2,3,0,1:T(8,128)}, f32[1,64,128,128]{2,3,0,1:T(8,128)}, f32[1,64,128,128]{2,3,0,1:T(8,128)}) fusion(f32[2,64,128,128]{2,3,0,1:T(8,128)S(1)} %fusion.24, f32[64,128]{1,0:T(8,128)S(1)} %copy-done.18, f32[64,128]{1,0:T(8,128)S(1)} %copy-done.20, ...), kind=kLoop, calls=%fused_computation.25 | loop fusion | flops 12582912 | bytes 33619968 | tf_op jit(solution)/shard_map/sub | solution.py:63
  324.6 6.3 %pad_maximum_fusion.2 = f32[2,64,128,128]{2,3,0,1:T(8,128)} fusion(f32[1,64,128,128]{2,3,0,1:T(8,128)} %get-tuple-element.47, f32[1,64,128,128]{2,3,0,1:T(8,128)S(1)} %get-tuple-element.46), kind=kLoop, calls=%fused_computation.17 | loop fusion | flops 2097152 | bytes 16777216 | tf_op jit(solution)/shard_map/stack | solution.py:61
  331.0 8.7 %copy.179 = f32[2,64,128,128]{3,1,0,2:T(8,128)} copy(f32[2,64,128,128]{2,3,0,1:T(8,128)} %pad_maximum_fusion.2) | data formatting | bytes 16777216 | tf_op jit(solution)/shard_map/stack | solution.py:61
  339.7 6.7 %bitcast_multiply_fusion = f32[32,128,128]{2,0,1:T(8,128)S(1)} fusion(f32[2,64,128,128]{3,1,0,2:T(8,128)} %copy.179, f32[1,32,64]{2,1,0:T(8,128)S(1)} %get-tuple-element.76, f32[1,32,64]{2,1,0:T(8,128)S(1)} %copy-done.22), kind=kOutput, calls=%fused_computation.62 | convolution fusion | flops 805834752 | bytes 10502144 | tf_op jit(solution)/shard_map/qka,qajc->kjc/dot_general | solution.py:41
  347.6 31.9 %all_to_all.91 = f32[4096,1,128]{2,1,0:T(1,128)S(1)} all-to-all(f32[4096,1,128]{2,1,0:T(1,128)S(1)} %bitcast.181), channel_id=1, replica_groups=mesh['dp'=4,'ctx'=32] {'ctx'}, dimensions={0} | all-to-all | bytes 4194304 | tf_op jit(solution)/shard_map/all_to_all | solution.py:173
  381.4 3.1 copy.183
  384.5 7.9 %pad_maximum_fusion = f32[2,64,128,128]{2,3,0,1:T(8,128)} fusion(f32[1,64,128,128]{2,3,0,1:T(8,128)} %get-tuple-element.62, f32[1,64,128,128]{2,3,0,1:T(8,128)} %get-tuple-element.63), kind=kLoop, calls=%fused_computation.6 | loop fusion | flops 2097152 | bytes 16777216 | tf_op jit(solution)/shard_map/stack | solution.py:61
  392.4 8.8 %copy.164 = f32[2,64,128,128]{3,1,0,2:T(8,128)} copy(f32[2,64,128,128]{2,3,0,1:T(8,128)} %pad_maximum_fusion) | data formatting | bytes 16777216 | tf_op jit(solution)/shard_map/stack | solution.py:61
  401.2 6.7 %bitcast_multiply_fusion.2 = f32[32,128,128]{2,0,1:T(8,128)S(1)} fusion(f32[2,64,128,128]{3,1,0,2:T(8,128)} %copy.164, f32[1,32,64]{2,1,0:T(8,128)S(1)} %get-tuple-element.76, f32[1,32,64]{2,1,0:T(8,128)S(1)} %copy-done.22), kind=kOutput, calls=%fused_computation.64 | convolution fusion | flops 805834752 | bytes 10502144 | tf_op jit(solution)/shard_map/qka,qajc->kjc/dot_general | solution.py:41
  407.9 2.6 copy.165
  410.5 4.3 all-to-all-start.2
  414.9 2.0 copy.185
  416.9 2.0 copy.186
  419.0 2.3 copy.190
  422.5 20.3 %all-to-all-done.2 = f32[4096,1,128]{2,1,0:T(1,128)S(1)} async-done(((f32[4096,1,128]{2,1,0:T(1,128)}), f32[4096,1,128]{2,1,0:T(1,128)S(1)}, u32[]{:S(2)}, u32[]{:S(2)}) %all-to-all-start.2) | async-done | bytes 2097184 | tf_op jit(solution)/shard_map/all_to_all | solution.py:171
  449.8 65.2 %all-reduce = (f32[]{:T(128)}, f32[]{:T(128)}) all-reduce(f32[]{:T(128)} %get-tuple-element.31, f32[]{:T(128)} %get-tuple-element.30), channel_id=1, replica_groups=mesh['dp'=4,'ctx'=32] {'dp','ctx'}, use_global_device_ids=true, to_apply=%region_4.5 | all-reduce | flops 2 | bytes 16 | tf_op jit(solution)/shard_map/psum | solution.py:184
  (99 shorter events, 40.5 us)
Async XLA Ops:
  9.1 2.0 copy-start.4
  14.0 37.5 %all-to-all-start = ((f32[128,32,128]{2,0,1:T(8,128)}), f32[128,32,128]{2,0,1:T(8,128)S(1)}, u32[]{:S(2)}, u32[]{:S(2)}) async-start(f32[128,32,128]{2,0,1:T(8,128)} %copy.153), calls=%async_computation | async-start | bytes 4194304 | tf_op jit(solution)/shard_map/all_to_all | solution.py:154
  25.3 5.6 %copy-start.5 = (bf16[1,128,4096]{1,2,0:T(8,128)(2,1)}, bf16[1,128,4096]{1,2,0:T(8,128)(2,1)S(1)}, u32[]{:S(2)}) copy-start(bf16[1,128,4096]{1,2,0:T(8,128)(2,1)S(1)} %copy.150) | copy-start | bytes 3145732
  51.5 34.7 %all-to-all-start.3 = ((f32[128,32,128]{2,0,1:T(8,128)}), f32[128,32,128]{2,0,1:T(8,128)}, u32[]{:S(2)}, u32[]{:S(2)}) async-start(f32[128,32,128]{2,0,1:T(8,128)} %copy.171), calls=%async_computation.3 | async-start | bytes 4194304 | tf_op jit(solution)/shard_map/all_to_all | solution.py:161
  60.0 26.1 %copy-start.23 = (f32[1,64,32]{1,2,0:T(8,128)}, f32[1,64,32]{1,2,0:T(8,128)S(1)}, u32[]{:S(2)}) copy-start(f32[1,64,32]{1,2,0:T(8,128)S(1)} %get-tuple-element.68) | copy-start | bytes 24580
  60.1 26.1 %copy-start.25 = (f32[1,64,32]{1,2,0:T(8,128)}, f32[1,64,32]{1,2,0:T(8,128)S(1)}, u32[]{:S(2)}) copy-start(f32[1,64,32]{1,2,0:T(8,128)S(1)} %get-tuple-element.69) | copy-start | bytes 24580
  73.8 21.4 %copy-start.13 = (f32[64,128]{0,1:T(8,128)S(1)}, f32[64,128]{0,1:T(8,128)}, u32[]{:S(2)}) copy-start(f32[64,128]{0,1:T(8,128)} %copy.155) | copy-start | bytes 98308
  73.8 21.4 %copy-start.15 = (f32[64,128]{0,1:T(8,128)S(1)}, f32[64,128]{0,1:T(8,128)}, u32[]{:S(2)}) copy-start(f32[64,128]{0,1:T(8,128)} %copy.156) | copy-start | bytes 98308
  86.2 9.0 %copy-start.2 = (f32[2,64,128,128]{3,1,2,0:T(8,128)S(1)}, f32[2,64,128,128]{3,1,2,0:T(8,128)}, u32[]{:S(2)}) copy-start(f32[2,64,128,128]{3,1,2,0:T(8,128)} %fusion.34) | copy-start | bytes 25165828
  105.1 3.5 copy-start.9
  126.4 18.3 %copy-start = (f32[2,64,128,128]{2,3,0,1:T(8,128)}, f32[2,64,128,128]{2,3,0,1:T(8,128)S(1)}, u32[]{:S(2)}) copy-start(f32[2,64,128,128]{2,3,0,1:T(8,128)S(1)} %fusion.15) | copy-start | bytes 25165828
  144.7 3.3 copy-start.1
  148.0 8.0 %copy-start.17 = (f32[64,128]{1,0:T(8,128)S(1)}, f32[64,128]{1,0:T(8,128)}, u32[]{:S(2)}) copy-start(f32[64,128]{1,0:T(8,128)} %get-tuple-element.74) | copy-start | bytes 98308
  148.0 8.0 %copy-start.19 = (f32[64,128]{1,0:T(8,128)S(1)}, f32[64,128]{1,0:T(8,128)}, u32[]{:S(2)}) copy-start(f32[64,128]{1,0:T(8,128)} %get-tuple-element.75) | copy-start | bytes 98308
  161.8 8.8 %copy-start.21 = (f32[1,32,64]{2,1,0:T(8,128)S(1)}, f32[1,32,64]{2,1,0:T(8,128)}, u32[]{:S(2)}) copy-start(f32[1,32,64]{2,1,0:T(8,128)} %get-tuple-element.77) | copy-start | bytes 24580
  179.9 34.0 %all-to-all-start.4 = ((f32[4096,1,128]{2,1,0:T(1,128)}), f32[4096,1,128]{2,1,0:T(1,128)S(1)}, u32[]{:S(2)}, u32[]{:S(2)}) async-start(f32[4096,1,128]{2,1,0:T(1,128)} %bitcast.174), calls=%async_computation.4 | async-start | bytes 4194304 | tf_op jit(solution)/shard_map/all_to_all | solution.py:172
  186.0 262.1 %reduce-scatter.2.cloned.1.call-start = ((), (), s32[]{:S(2)}) async-start(), calls=%async_computation.7 | async-start | bytes 2621440 | tf_op jit(solution)/shard_map/reduce_scatter | solution.py:178
  215.8 1.9 copy-start.8
  219.7 36.4 %copy-start.24 = (f32[1,64,32]{1,2,0:T(8,128)S(1)}, f32[1,64,32]{1,2,0:T(8,128)}, u32[]{:S(2)}) copy-start(f32[1,64,32]{1,2,0:T(8,128)} %copy-done.23) | copy-start | bytes 24580
  219.7 36.4 %copy-start.26 = (f32[1,64,32]{1,2,0:T(8,128)S(1)}, f32[1,64,32]{1,2,0:T(8,128)}, u32[]{:S(2)}) copy-start(f32[1,64,32]{1,2,0:T(8,128)} %copy-done.25) | copy-start | bytes 24580
  256.1 7.2 %copy-start.14 = (f32[64,128]{0,1:T(8,128)S(1)}, f32[64,128]{0,1:T(8,128)}, u32[]{:S(2)}) copy-start(f32[64,128]{0,1:T(8,128)} %copy.155) | copy-start | bytes 98308
  256.1 7.2 %copy-start.16 = (f32[64,128]{0,1:T(8,128)S(1)}, f32[64,128]{0,1:T(8,128)}, u32[]{:S(2)}) copy-start(f32[64,128]{0,1:T(8,128)} %copy.156) | copy-start | bytes 98308
  266.2 4.2 copy-start.10
  266.2 23.7 %slice-start = ((s8[8388608]{0:T(1024)(128)(4,1)}), s8[4194304]{0:T(1024)(128)(4,1)S(1)}, s32[]{:S(2)}) async-start(s8[8388608]{0:T(1024)(128)(4,1)} %bitcast.168), calls=%async_computation.8 | async-start | bytes 8388608
  270.4 19.5 %slice-start.1 = ((s8[8388608]{0:T(1024)(128)(4,1)}), s8[4194304]{0:T(1024)(128)(4,1)S(1)}, s32[]{:S(2)}) async-start(s8[8388608]{0:T(1024)(128)(4,1)} %bitcast.168), calls=%async_computation.9 | async-start | bytes 8388608
  301.0 9.4 %copy-start.3 = (f32[1,64,128,128]{2,3,0,1:T(8,128)S(1)}, f32[1,64,128,128]{2,3,0,1:T(8,128)}, u32[]{:S(2)}) copy-start(f32[1,64,128,128]{2,3,0,1:T(8,128)} %get-tuple-element.35) | copy-start | bytes 12582916
  310.4 8.1 %copy-start.18 = (f32[64,128]{1,0:T(8,128)S(1)}, f32[64,128]{1,0:T(8,128)}, u32[]{:S(2)}) copy-start(f32[64,128]{1,0:T(8,128)} %get-tuple-element.74) | copy-start | bytes 98308
  310.4 8.1 %copy-start.20 = (f32[64,128]{1,0:T(8,128)S(1)}, f32[64,128]{1,0:T(8,128)}, u32[]{:S(2)}) copy-start(f32[64,128]{1,0:T(8,128)} %get-tuple-element.75) | copy-start | bytes 98308
  331.0 8.7 %copy-start.22 = (f32[1,32,64]{2,1,0:T(8,128)S(1)}, f32[1,32,64]{2,1,0:T(8,128)}, u32[]{:S(2)}) copy-start(f32[1,32,64]{2,1,0:T(8,128)} %get-tuple-element.77) | copy-start | bytes 24580
  410.5 10.7 %copy-start.7 = (bf16[1,128,4096]{1,2,0:T(8,128)(2,1)S(1)}, bf16[1,128,4096]{1,2,0:T(8,128)(2,1)}, u32[]{:S(2)}) copy-start(bf16[1,128,4096]{1,2,0:T(8,128)(2,1)} %get-tuple-element.54) | copy-start | bytes 3145732
  410.5 32.3 %all-to-all-start.2 = ((f32[4096,1,128]{2,1,0:T(1,128)}), f32[4096,1,128]{2,1,0:T(1,128)S(1)}, u32[]{:S(2)}, u32[]{:S(2)}) async-start(f32[4096,1,128]{2,1,0:T(1,128)} %bitcast.172), calls=%async_computation.2 | async-start | bytes 4194304 | tf_op jit(solution)/shard_map/all_to_all | solution.py:171
  442.8 3.7 copy-start.6
  446.5 69.9 %copy-start.11 = (f32[128,1024]{0,1:T(8,128)S(1)}, f32[128,1024]{0,1:T(8,128)}, u32[]{:S(2)}) copy-start(f32[128,1024]{0,1:T(8,128)} %copy.185) | copy-start | bytes 1572868
  446.5 69.9 %copy-start.12 = (f32[128,1024]{0,1:T(8,128)S(1)}, f32[128,1024]{0,1:T(8,128)}, u32[]{:S(2)}) copy-start(f32[128,1024]{0,1:T(8,128)} %copy.186) | copy-start | bytes 1572868
Sparse Core Ops, SparseCore 0:
  384.7 27.0 reduce-scatter.1
where the time goes:
time: 536 us; the launch traced here: 528 us
  blocking collectives  132 us (25%)
  matrix products  128 us (24%)
  local copies, waits for them, and re-layouts  81.7 us (15%)
  waiting for transfers between devices  74.3 us (14%)
  other arithmetic  70 us (13%)
  starting transfers between devices  26.8 us (5%)
  between operations  16.1 us (3%)
    dot_general x6, matrix products, middle_section(): return jnp.einsum('rqmj,qkjc->rkmc', table, stacked, precision=highest)  81 us
    psum x1, blocking collectives, on_device(): total_sq, bad_count = lax.psum((local_square, local_bad), ('dp', 'ctx'))  65.2 us
    all_to_all x1, blocking collectives, on_device(): lax.all_to_all(group_order(mixed_in, data_count, part_count, sub_width),...  34.5 us
    all_to_all x1, blocking collectives, on_device(): lax.all_to_all(arrived[2], 'ctx', split_axis=0, concat_axis=1, tiled=True)  31.9 us
    another operation x6, other arithmetic, rotate(): jnp.stack([real_part * cosine_table - imaginary * sine_table, real_part *...  28.9 us
    dot_general x3, matrix products, lead_forward(): return jnp.einsum('rka,ajc->rkjc', table, values, precision=highest)  26.6 us
    another operation x3, local copies, waits for them, and re-layouts, rotate(): jnp.stack([real_part * cosine_table - imaginary * sine_table, real_part *...  26.3 us
    all_to_all x1, waiting for transfers between devices, on_device(): lax.all_to_all(arrived[1], 'ctx', split_axis=0, concat_axis=1, tiled=True)  23.8 us
  transfers between devices with their start and end apart: 5, of which 4 were waited for; matrix products, arithmetic and copies ran while one was open for 13% of the time, Pallas kernels for 0%

commit v1 on v0

v1 whole, which is shorter than its diff:
```python
import functools
import math

import jax
import jax.numpy as jnp
import numpy as np
from jax import lax
from jax.experimental import pallas as pl
from jax.experimental.pallas import tpu as pltpu
from jax.sharding import PartitionSpec as P

MESH = pl.DeviceIdType.MESH
F32 = jnp.float32
BF16 = jnp.bfloat16

DP = 4
CTX = 32
ROWS = 128
LANES = 128
PERIOD = CTX * ROWS

beta_first = 0.9
beta_second = 0.95
learn_rate = 0.01
decay_rate = 0.1
adam_epsilon = 1e-08
correct_first = 0.9999734386011124
correct_second = 0.994079470779666


def dft_tables():
    k1 = np.arange(CTX)[:, None, None]
    m = np.arange(ROWS)[None, :, None]
    j = np.arange(ROWS)[None, None, :]
    turns = (j * (4 * k1 + 1 + 4 * CTX * m)) % (4 * PERIOD)
    angle = turns * (2.0 * np.pi / (4 * PERIOD))
    cosine, sine = np.cos(angle), np.sin(angle)
    forward = np.concatenate([cosine, sine], axis=2)
    inverse = np.concatenate([cosine.swapaxes(1, 2), sine.swapaxes(1, 2)], axis=2) / PERIOD
    out = []
    for table in (forward, inverse):
        high = table.astype(jnp.bfloat16)
        low = (table - high.astype(np.float64)).astype(jnp.bfloat16)
        out += [high, low]
    return np.stack(out)


def rotated(value, turn):
    re, im = value
    turn = turn % 1.0
    if turn == 0.0:
        return value
    c, s = math.cos(2 * math.pi * turn), math.sin(2 * math.pi * turn)
    return (re * c + im * s, im * c - re * s)


def dft8(v, sign):
    half = math.sqrt(0.5)

    def add(a, b):
        return (a[0] + b[0], a[1] + b[1])

    def sub(a, b):
        return (a[0] - b[0], a[1] - b[1])

    def quarter(a):
        return (a[1], -a[0]) if sign > 0 else (-a[1], a[0])

    def sub_quarter(a, b):
        if sign > 0:
            return (a[0] + b[1], a[1] - b[0]), (a[0] - b[1], a[1] + b[0])
        return (a[0] - b[1], a[1] + b[0]), (a[0] + b[1], a[1] - b[0])

    def dft4(a, b, c, d):
        s0, s1 = add(a, c), sub(a, c)
        s2, s3 = add(b, d), sub(b, d)
        y1, y3 = sub_quarter(s1, s3)
        return add(s0, s2), y1, sub(s0, s2), y3

    e = dft4(v[0], v[2], v[4], v[6])
    o = dft4(v[1], v[3], v[5], v[7])
    if sign > 0:
        o1 = ((o[1][0] + o[1][1]) * half, (o[1][1] - o[1][0]) * half)
        o3 = ((o[3][1] - o[3][0]) * half, (o[3][0] + o[3][1]) * (-half))
    else:
        o1 = ((o[1][0] - o[1][1]) * half, (o[1][1] + o[1][0]) * half)
        o3 = ((o[3][0] + o[3][1]) * (-half), (o[3][0] - o[3][1]) * half)
    y2, y6 = sub_quarter(e[2], o[2])
    return [
        add(e[0], o[0]), add(e[1], o1), y2, add(e[3], o3),
        sub(e[0], o[0]), sub(e[1], o1), y6, sub(e[3], o3),
    ]


def lead_forward(x):
    c1, s1 = math.cos(math.pi / 8), math.sin(math.pi / 8)
    half = math.sqrt(0.5)
    u = [[None] * 8 for _ in range(4)]
    for a0 in range(8):
        x0, x1, x2, x3 = x[a0], x[a0 + 8], x[a0 + 16], x[a0 + 24]
        p1r, p1i = x1 * c1, x1 * s1
        p3r, p3i = x3 * s1, x3 * c1
        s = x2 * half
        ep, em = x0 + s, x0 - s
        sr, si = p1r + p3r, p1i + p3i
        dr, di = p1r - p3r, p1i - p3i
        u[0][a0] = (ep + sr, -(s + si))
        u[2][a0] = (ep - sr, si - s)
        u[1][a0] = (em - di, s - dr)
        u[3][a0] = (em + di, s + dr)
    out = [None] * 32
    for q in range(4):
        y = dft8([rotated(u[q][a0], a0 * (4 * q + 1) / 128.0) for a0 in range(8)], 1)
        for r in range(8):
            out[q + 4 * r] = y[r]
    return out


def lead_inverse(v):
    c1, s1 = math.cos(math.pi / 8), math.sin(math.pi / 8)
    half = math.sqrt(0.5)
    u = []
    for q in range(4):
        t = dft8([v[q + 4 * r] for r in range(8)], -1)
        u.append([rotated(t[a0], -a0 * (4 * q + 1) / 128.0) for a0 in range(8)])
    out = [None] * 32
    for a0 in range(8):
        (r0, i0), (r1, i1), (r2, i2), (r3, i3) = u[0][a0], u[1][a0], u[2][a0], u[3][a0]
        ar, ai, br, bi = r0 + r2, i0 + i2, r0 - r2, i0 - i2
        cr, ci, dr, di = r1 + r3, i1 + i3, r1 - r3, i1 - i3
        out[a0] = ar + cr
        out[a0 + 8] = (br - di) * c1 - (bi + dr) * s1
        out[a0 + 16] = ((ar - cr) - (ai - ci)) * half
        out[a0 + 24] = (br + di) * s1 - (bi - dr) * c1
    return out


def owner_plane(ctx):
    z, y, core = ctx // 8, (ctx // 2) % 4, ctx % 2
    return 2 * ((z + y) % 2) + core


def owner_slot(ctx):
    z, y = ctx // 8, (ctx // 2) % 4
    return 2 * z + y // 2


def channel_block(ctx):
    return owner_plane(ctx) * 8 + owner_slot(ctx)


def summing_level(plane):
    return 2 * (plane % 2) + (1 - plane // 2)


def split(value):
    high = value.astype(BF16)
    return high, (value - high.astype(F32)).astype(BF16)


def times_table(table, kind, k1, re, im):
    wide = jnp.concatenate([re, im], axis=1)
    high, low = split(wide)

    def paired(part):
        other = jnp.concatenate([part[:, LANES:], -part[:, :LANES]], axis=1)
        return jnp.concatenate([part, other], axis=0)

    high, low = paired(high), paired(low)
    t_high, t_low = table[kind, k1], table[kind + 1, k1]
    dot = functools.partial(jnp.dot, preferred_element_type=F32)
    return dot(t_high, high) + dot(t_low, high) + dot(t_high, low)


def body(
    q_hbm, k_hbm, v_hbm, g_hbm, filt_hbm, m1_hbm, m2_hbm, tab_hbm,
    qg_hbm, kg_hbm, vg_hbm, nf_hbm, n1_hbm, n2_hbm,
    q_in, k_in, v_in, g_in, filt_part, filt_own, m1, m2, tab,
    send_m, send_g, send_b, got_m, got_k, got_g, work, spec_k, spec_m, spec_g,
    got_conv, got_back, parts, summed, lag,
    tile_mine, tile_x, tile_row, tile_all,
    load_sem, out_sem, ksend, krecv, kxsend, kxrecv, msend, mrecv, gsend, grecv,
    csend, crecv, bsend, brecv, psend, precv, lsend, lrecv, xsend, xrecv, asend, arecv, own_sem,
):
    d = lax.axis_index("dp")
    c = lax.axis_index("ctx")
    plane = owner_plane(c)
    slot = owner_slot(c)
    mine = channel_block(c)
    z, y = c // 8, (c // 2) % 4

    loads = {}
    def load(name, index, source, target):
        loads[name] = pltpu.make_async_copy(source, target, load_sem.at[index])
        loads[name].start()

    load("filt", 0, filt_hbm.at[pl.ds(pl.multiple_of(d * 32, 32), 32)], filt_part)
    load("k", 1, k_hbm.at[0], k_in)
    load("v", 2, v_hbm.at[0], v_in)
    load("g", 3, g_hbm.at[0], g_in)
    load("q", 4, q_hbm.at[0], q_in)
    load("tab", 5, tab_hbm, tab)
    load("own", 6, filt_hbm.at[:, pl.ds(pl.multiple_of(d * 1024, 1024), 1024)], filt_own)
    load("m1", 7, m1_hbm, m1)
    load("m2", 8, m2_hbm, m2)

    level = (z + y) % 4
    helper = 2 * (1 - level % 2) + level // 2

    def lag_source(h):
        hz = h // 2
        hy = 2 * (h % 2) + (d // 2 + hz) % 2
        return hz * 8 + hy * 2 + d % 2

    def lag_target(i, of_plane):
        tz = i // 2
        ty = (summing_level(of_plane) - tz + 4) % 4
        return tz * 8 + ty * 2 + i % 2

    barrier = pltpu.get_barrier_semaphore()

    def greet(i, carry):
        pl.semaphore_signal(barrier, inc=1, device_id=(d, (c + i) % CTX), device_id_type=MESH)
        return carry

    lax.fori_loop(1, CTX, greet, 0)
    for step in range(1, DP):
        pl.semaphore_signal(barrier, inc=1, device_id=((d + step) % DP, c), device_id_type=MESH)

    def greet_lag(h, carry):
        pl.semaphore_signal(barrier, inc=1, device_id=(helper, lag_source(h)), device_id_type=MESH)
        return carry

    lax.fori_loop(0, 8, greet_lag, 0)
    pl.semaphore_wait(barrier, 31 + 3 + 8)

    def peer(i):
        return (c + i) % CTX

    def wait_bytes(ref, sem):
        pltpu.make_async_copy(ref, ref, sem).wait()

    quarter = pl.ds(pl.multiple_of(d * 32, 32), 32)

    def filt_cols(block):
        return filt_part.at[:, pl.ds(pl.multiple_of(block * LANES, LANES), LANES)]

    loads["filt"].wait()

    def send_filter(i, carry):
        t = peer(i)
        pltpu.make_async_remote_copy(
            src_ref=filt_cols(channel_block(t)), dst_ref=got_k.at[c, quarter],
            send_sem=ksend, recv_sem=krecv, device_id=(d, t), device_id_type=MESH,
        ).start()
        return carry

    lax.fori_loop(1, CTX, send_filter, 0)
    own_copy = pltpu.make_async_copy(filt_cols(mine), got_k.at[c, quarter], own_sem)
    own_copy.start()

    def product_out(left, right, store, target, ssem, rsem):
        def block(i, carry):
            t = peer(i)
            b = channel_block(t)
            cols = pl.ds(pl.multiple_of(b * LANES, LANES), LANES)
            store[b] = left[:, cols].astype(F32) * right[:, cols].astype(F32)
            pltpu.make_async_remote_copy(
                src_ref=store.at[b], dst_ref=target.at[c],
                send_sem=ssem, recv_sem=rsem, device_id=(d, t), device_id_type=MESH,
            ).start()
            return carry

        lax.fori_loop(1, CTX, block, 0)
        cols = pl.ds(pl.multiple_of(mine * LANES, LANES), LANES)
        target[c] = left[:, cols].astype(F32) * right[:, cols].astype(F32)

    loads["k"].wait()
    loads["v"].wait()
    product_out(k_in, v_in, send_m, got_m, msend, mrecv)

    own_copy.wait()
    wait_bytes(got_k.at[pl.ds(0, 31), quarter], krecv)
    share = []
    for step in range(1, DP):
        copy = pltpu.make_async_remote_copy(
            src_ref=got_k.at[:, quarter], dst_ref=got_k.at[:, quarter],
            send_sem=kxsend.at[step - 1], recv_sem=kxrecv.at[step - 1],
            device_id=((d + step) % DP, c), device_id_type=MESH,
        )
        copy.start()
        share.append(copy)

    loads["g"].wait()
    loads["q"].wait()
    product_out(g_in, q_in, send_g, got_g, gsend, grecv)

    def forward(got, spec, scale=None):
        def lead(i, carry):
            rows = pl.ds(pl.multiple_of(i * 8, 8), 8)
            x = [got[a, rows] for a in range(CTX)]
            if scale is not None:
                x = [value * scale for value in x]
            for k1, (re, im) in enumerate(lead_forward(x)):
                work[k1, rows, :LANES] = re
                work[k1, rows, LANES:] = im
            return carry

        lax.fori_loop(0, ROWS // 8, lead, 0)

        def rest(i, carry):
            for k1 in (2 * i, 2 * i + 1):
                spec[k1] = times_table(tab, 0, k1, work[k1, :, :LANES], work[k1, :, LANES:])
            return carry

        lax.fori_loop(0, CTX // 2, rest, 0)

    def inverse(left, right, conjugate, out):
        def rest(i, carry):
            for k1 in (2 * i, 2 * i + 1):
                lr, li = left[k1, :, :LANES], left[k1, :, LANES:]
                rr, ri = right[k1, :, :LANES], right[k1, :, LANES:]
                if conjugate:
                    re, im = lr * rr + li * ri, li * rr - lr * ri
                else:
                    re, im = lr * rr - li * ri, -(lr * ri + li * rr)
                work[k1] = times_table(tab, 2, k1, re, im)
            return carry

        lax.fori_loop(0, CTX // 2, rest, 0)

        def lead(i, carry):
            rows = pl.ds(pl.multiple_of(i * 8, 8), 8)
            v = [(work[k1, rows, :LANES], -work[k1, rows, LANES:]) for k1 in range(CTX)]
            for a, value in enumerate(lead_inverse(v)):
                out[a, rows] = value
            return carry

        lax.fori_loop(0, ROWS // 8, lead, 0)

    def send_back(source, target, ssem, rsem):
        def block(i, carry):
            t = peer(i)
            pltpu.make_async_remote_copy(
                src_ref=source.at[t], dst_ref=target.at[mine],
                send_sem=ssem, recv_sem=rsem, device_id=(d, t), device_id_type=MESH,
            ).start()
            return carry

        lax.fori_loop(1, CTX, block, 0)
        copy = pltpu.make_async_copy(source.at[c], target.at[mine], own_sem)
        copy.start()
        return copy

    blocks = pl.ds(0, CTX - 1)
    loads["tab"].wait()
    wait_bytes(got_m.at[blocks], mrecv)
    forward(got_m, spec_m)
    for copy in share:
        copy.wait()
    forward(got_k, spec_k, PERIOD**-0.5)
    wait_bytes(send_m.at[blocks], msend)
    inverse(spec_k, spec_m, False, send_m)
    conv_own = send_back(send_m, got_conv, csend, crecv)

    wait_bytes(got_g.at[blocks], grecv)
    forward(got_g, spec_g)
    wait_bytes(send_g.at[blocks], gsend)
    inverse(spec_m, spec_g, True, send_g)

    share = []
    for step in range(1, DP):
        to = (d + step) % DP
        for pair in range(4):
            copy = pltpu.make_async_remote_copy(
                src_ref=send_g.at[pl.ds(lag_target(2 * pair, to), 2)],
                dst_ref=parts.at[step - 1, pl.ds(2 * pair, 2)],
                send_sem=psend.at[step - 1, pair], recv_sem=precv.at[step - 1, pair],
                device_id=(to, c), device_id_type=MESH,
            )
            copy.start()
            share.append(copy)

    inverse(spec_k, spec_g, True, send_b)
    conv_own.wait()
    back_own = send_back(send_b, got_back, bsend, brecv)

    wait_bytes(got_conv.at[blocks], crecv)

    def finish_conv(b, carry):
        cols = pl.ds(pl.multiple_of(b * LANES, LANES), LANES)
        q_in[:, cols] = (g_in[:, cols].astype(F32) * got_conv[b]).astype(BF16)
        return carry

    lax.fori_loop(0, CTX, finish_conv, 0)
    outs = []

    def write_out(index, source, target):
        copy = pltpu.make_async_copy(source, target, out_sem.at[index])
        copy.start()
        outs.append(copy)

    write_out(0, q_in, qg_hbm.at[0])

    for copy in share:
        copy.wait()

    def add_up(i, carry):
        t = lag_target(i, d)
        summed[i] = (send_g[t] + parts[0, i]) + (parts[1, i] + parts[2, i])
        pltpu.make_async_remote_copy(
            src_ref=summed.at[i], dst_ref=lag.at[slot],
            send_sem=lsend, recv_sem=lrecv, device_id=(plane, t), device_id_type=MESH,
        ).start()
        return carry

    lax.fori_loop(0, 8, add_up, 0)
    wait_bytes(lag, lrecv)

    def measure(i, carry):
        squares, bad = carry
        value = lag[i].reshape(16, 8, LANES)
        finite = jnp.abs(value) < jnp.inf
        return (
            squares + jnp.sum(value * value, axis=0),
            bad + jnp.sum(jnp.where(finite, 0.0, 1.0), axis=0),
        )

    nothing = jnp.zeros((8, LANES), F32)
    squares, bad = lax.fori_loop(0, 8, measure, (nothing, nothing))
    tile_mine[:8] = squares
    tile_mine[8:] = bad
    share = []
    for step in range(1, DP):
        copy = pltpu.make_async_remote_copy(
            src_ref=tile_mine, dst_ref=tile_x.at[step - 1],
            send_sem=xsend.at[step - 1], recv_sem=xrecv.at[step - 1],
            device_id=((d + step) % DP, c), device_id_type=MESH,
        )
        copy.start()
        share.append(copy)
    for copy in share:
        copy.wait()
    tile_row[...] = (tile_mine[...] + tile_x[0]) + (tile_x[1] + tile_x[2])

    def spread(i, carry):
        pltpu.make_async_remote_copy(
            src_ref=tile_row, dst_ref=tile_all.at[c],
            send_sem=asend, recv_sem=arecv, device_id=(d, peer(i)), device_id_type=MESH,
        ).start()
        return carry

    lax.fori_loop(1, CTX, spread, 0)
    tile_all[c] = tile_row[...]

    back_own.wait()
    wait_bytes(got_back.at[blocks], brecv)

    def finish_back(b, carry):
        cols = pl.ds(pl.multiple_of(b * LANES, LANES), LANES)
        back = got_back[b]
        keys, values = k_in[:, cols].astype(F32), v_in[:, cols].astype(F32)
        v_in[:, cols] = (back * values).astype(BF16)
        k_in[:, cols] = (back * keys).astype(BF16)
        return carry

    lax.fori_loop(0, CTX, finish_back, 0)
    write_out(1, v_in, kg_hbm.at[0])
    write_out(2, k_in, vg_hbm.at[0])

    wait_bytes(tile_all.at[blocks], arecv)
    everything = jnp.sum(tile_all[...], axis=0)
    total_sq = jnp.sum(everything[:8])
    bad_count = jnp.sum(everything[8:])
    mean_sq = jnp.full((8, LANES), total_sq) * (1.0 / (PERIOD * 4096)) + 1e-06
    factor = jnp.minimum(1.0, 1.0 / jnp.sqrt(mean_sq))[:1]
    commit = (jnp.full((8, LANES), bad_count) == 0.0)[:1]
    loads["own"].wait()
    loads["m1"].wait()
    loads["m2"].wait()

    def step(h, carry):
        cols = pl.ds(pl.multiple_of(h * LANES, LANES), LANES)
        clipped = lag[h] * factor
        first, second, weight = m1[:, cols], m2[:, cols], filt_own[:, cols]
        first_next = beta_first * first + (1.0 - beta_first) * clipped
        second_next = beta_second * second + (1.0 - beta_second) * clipped * clipped
        update = (
            first_next / correct_first / (jnp.sqrt(second_next / correct_second) + adam_epsilon)
            + decay_rate * weight
        )
        filt_own[:, cols] = jnp.where(commit, weight - learn_rate * update, weight)
        m1[:, cols] = jnp.where(commit, first_next, first)
        m2[:, cols] = jnp.where(commit, second_next, second)
        return carry

    lax.fori_loop(0, 8, step, 0)
    write_out(3, filt_own, nf_hbm)
    write_out(4, m1, n1_hbm)
    write_out(5, m2, n2_hbm)

    wait_bytes(got_k.at[blocks, quarter], ksend)
    wait_bytes(send_m.at[blocks], csend)
    wait_bytes(send_b.at[blocks], bsend)
    wait_bytes(summed, lsend)
    wait_bytes(tile_all.at[blocks], asend)
    for copy in outs:
        copy.wait()


def on_device(query_act, key_act, value_act, out_grad, filter_weight, first_moment, second_moment):
    table = jnp.asarray(dft_tables())
    block = (CTX, ROWS, LANES)
    wide = (CTX, ROWS, 2 * LANES)
    vmem = pltpu.VMEM
    dma = pltpu.SemaphoreType.DMA
    anywhere = pl.BlockSpec(memory_space=pl.ANY)
    stream = jax.ShapeDtypeStruct(query_act.shape, BF16)
    state = jax.ShapeDtypeStruct(first_moment.shape, F32)
    return pl.pallas_call(
        body,
        out_shape=(stream, stream, stream, state, state, state),
        in_specs=[anywhere] * 8,
        out_specs=(anywhere,) * 6,
        scratch_shapes=[
            vmem((ROWS, 4096), BF16), vmem((ROWS, 4096), BF16),
            vmem((ROWS, 4096), BF16), vmem((ROWS, 4096), BF16),
            vmem((32, 4096), F32), vmem((ROWS, 1024), F32),
            vmem((ROWS, 1024), F32), vmem((ROWS, 1024), F32),
            vmem((4,) + wide, BF16),
            vmem(block, F32), vmem(block, F32), vmem(block, F32),
            vmem(block, F32), vmem(block, F32), vmem(block, F32),
            vmem(wide, F32), vmem(wide, F32), vmem(wide, F32), vmem(wide, F32),
            vmem(block, F32), vmem(block, F32),
            vmem((3, 8, ROWS, LANES), F32), vmem((8, ROWS, LANES), F32), vmem((8, ROWS, LANES), F32),
            vmem((16, LANES), F32), vmem((3, 16, LANES), F32), vmem((16, LANES), F32),
            vmem((CTX, 16, LANES), F32),
            dma((9,)), dma((6,)), dma, dma, dma((3,)), dma((3,)), dma, dma, dma, dma,
            dma, dma, dma, dma, dma((3, 4)), dma((3, 4)), dma, dma, dma((3,)), dma((3,)), dma, dma, dma,
        ],
        compiler_params=pltpu.CompilerParams(
            collective_id=0, has_side_effects=True, vmem_limit_bytes=60 * 2**20
        ),
    )(query_act, key_act, value_act, out_grad, filter_weight, first_moment, second_moment, table)


def solution(mesh):
    return jax.shard_map(
        on_device,
        mesh=mesh,
        in_specs=(
            P("dp", "ctx", None),
            P("dp", "ctx", None),
            P("dp", "ctx", None),
            P("dp", "ctx", None),
            P("ctx", None),
            P("ctx", "dp"),
            P("ctx", "dp"),
        ),
        out_specs=(
            P("dp", "ctx", None),
            P("dp", "ctx", None),
            P("dp", "ctx", None),
            P("ctx", "dp"),
            P("ctx", "dp"),
            P("ctx", "dp"),
        ),
        check_vma=False,
    )
```

time: 536 us -> 166 us (0.31); the launches traced: 528 us -> 165 us
  Pallas kernels: 0 us -> 153 us
  blocking collectives: 132 us -> 0 us
  matrix products: 128 us -> 0 us
  waiting for transfers between devices: 74.3 us -> 0 us
  local copies, waits for them, and re-layouts: 81.7 us -> 11.5 us
  other arithmetic: 70 us -> 0 us
  starting transfers between devices: 26.8 us -> 0 us
  between operations: 16.1 us -> 0.65 us
    pallas_call x0 -> x1, Pallas kernels: none -> 153 us  [on_device(): pl.pallas_call(body, out_shape=(stream, stream, stream, state, state, sta...]
    dot_general x12 -> x0, matrix products: 128 us -> none  [the longest x6 81 us: middle_section(): return jnp.einsum('rqmj,qkjc->rkmc', table, stacked, precision=highest)]
    all_to_all x4 -> x0, waiting for transfers between devices: 74.3 us -> none  [the longest x1 23.8 us: on_device(): lax.all_to_all(arrived[1], 'ctx', split_axis=0, concat_axis=1, tiled=True)]
    all_to_all x2 -> x0, blocking collectives: 66.4 us -> none  [the longest x1 34.5 us: on_device(): lax.all_to_all(group_order(mixed_in, data_count, part_count, sub_width),...]
    psum x1 -> x0, blocking collectives: 65.2 us -> none  [on_device(): total_sq, bad_count = lax.psum((local_square, local_bad), ('dp', 'ctx'))]
    another operation x8 -> x0, other arithmetic: 29.6 us -> none  [the longest x6 28.9 us: rotate(): jnp.stack([real_part * cosine_table - imaginary * sine_table, real_part *...]
    all_to_all x4 -> x0, starting transfers between devices: 26.7 us -> none  [the longest x1 9.6 us: on_device(): lax.all_to_all(group_order(kernel, data_count, part_count, sub_width), 'c...]
    another operation x3 -> x0, local copies, waits for them, and re-layouts: 26.3 us -> none  [rotate(): jnp.stack([real_part * cosine_table - imaginary * sine_table, real_part *...]
  transfers between devices with their start and end apart: 5 -> 0, of which waited for: 4 -> 0; matrix products, arithmetic and copies ran while one was open for 13% -> 0% of each run, Pallas kernels for 0% -> 0%
where the time goes in v1:
time: 166 us; the launch traced here: 165 us
  Pallas kernels  153 us (92%)
  local copies, waits for them, and re-layouts  11.5 us (7%)
    pallas_call x1, Pallas kernels, on_device(): pl.pallas_call(body, out_shape=(stream, stream, stream, state, state, sta...  153 us
    unnamed x8, local copies, waits for them, and re-layouts  11.5 us

profile of v1, /device:TPU:1, one launch (start us, length us, event | category | flops | bytes accessed | tf_op | source)
XLA Modules:
  0.0 165.2 jit_solution(5294019714738572088)
XLA Ops:
  0.6 153.1 %shard_map.127 = (bf16[1,128,4096]{2,1,0:T(8,128)(2,1)}, bf16[1,128,4096]{2,1,0:T(8,128)(2,1)}, bf16[1,128,4096]{2,1,0:T(8,128)(2,1)}, f32[128,1024]{1,0:T(8,128...) custom-call(bf16[1,128,4096]{2,1,0:T(8,128)(2,1)} %q_hbm.1, bf16[1,128,4096]{2,1,0:T(8,128)(2,1)} %k_hbm.1, ...), custom_call_target="tpu_custom_call" | custom-call | tf_op jit(solution)/shard_map/pallas_call | solution.py:520
  153.7 0.0 copy-start
  153.7 2.3 %copy.20 = bf16[1,128,4096]{2,1,0:T(8,128)(2,1)} copy(bf16[1,128,4096]{2,1,0:T(8,128)(2,1)} %get-tuple-element.12) | data formatting | bytes 2097152
  156.1 2.3 %copy.21 = bf16[1,128,4096]{2,1,0:T(8,128)(2,1)} copy(bf16[1,128,4096]{2,1,0:T(8,128)(2,1)} %get-tuple-element.13) | data formatting | bytes 2097152
  158.3 2.3 %copy.22 = bf16[1,128,4096]{2,1,0:T(8,128)(2,1)} copy(bf16[1,128,4096]{2,1,0:T(8,128)(2,1)} %get-tuple-element.14) | data formatting | bytes 2097152
  160.6 1.9 %copy.23 = f32[128,1024]{1,0:T(8,128)} copy(f32[128,1024]{1,0:T(8,128)} %get-tuple-element.15) | data formatting | bytes 1048576
  162.5 1.9 %copy.24 = f32[128,1024]{1,0:T(8,128)} copy(f32[128,1024]{1,0:T(8,128)} %get-tuple-element.16) | data formatting | bytes 1048576
  164.4 0.0 copy-done
  164.4 0.8 copy.25
Async XLA Ops:
  153.7 10.7 %copy-start = (f32[128,1024]{1,0:T(8,128)S(1)}, f32[128,1024]{1,0:T(8,128)}, u32[]{:S(2)}) copy-start(f32[128,1024]{1,0:T(8,128)} %get-tuple-element.17) | copy-start | bytes 1572868

commit v2 on v1

--- a/solution.py
+++ b/solution.py
@@ -17,7 +17,12 @@
 CTX = 32
 ROWS = 128
 LANES = 128
+VMEM_MIB = 60
 PERIOD = CTX * ROWS
+STEPS = (
+    (2, 2), (2, 3), (3, 2), (2, 1), (1, 2), (2, 0), (0, 2), (1, 1),
+    (3, 3), (1, 3), (3, 1), (0, 1), (1, 0), (0, 3), (3, 0),
+)
 
 beta_first = 0.9
 beta_second = 0.95
@@ -173,11 +178,11 @@
 
 
 def body(
-    q_hbm, k_hbm, v_hbm, g_hbm, filt_hbm, m1_hbm, m2_hbm, tab_hbm,
-    qg_hbm, kg_hbm, vg_hbm, nf_hbm, n1_hbm, n2_hbm,
-    q_in, k_in, v_in, g_in, filt_part, filt_own, m1, m2, tab,
+    q_hbm, k_hbm, v_hbm, g_hbm, filt_hbm, tab_hbm,
+    qg_hbm, got_back, lag_hbm, total_ref,
+    q_in, k_in, v_in, g_in, filt_part, tab,
     send_m, send_g, send_b, got_m, got_k, got_g, work, spec_k, spec_m, spec_g,
-    got_conv, got_back, parts, summed, lag,
+    got_conv, parts, summed, lag,
     tile_mine, tile_x, tile_row, tile_all,
     load_sem, out_sem, ksend, krecv, kxsend, kxrecv, msend, mrecv, gsend, grecv,
     csend, crecv, bsend, brecv, psend, precv, lsend, lrecv, xsend, xrecv, asend, arecv, own_sem,
@@ -200,9 +205,6 @@
     load("g", 3, g_hbm.at[0], g_in)
     load("q", 4, q_hbm.at[0], q_in)
     load("tab", 5, tab_hbm, tab)
-    load("own", 6, filt_hbm.at[:, pl.ds(pl.multiple_of(d * 1024, 1024), 1024)], filt_own)
-    load("m1", 7, m1_hbm, m1)
-    load("m2", 8, m2_hbm, m2)
 
     level = (z + y) % 4
     helper = 2 * (1 - level % 2) + level // 2
@@ -234,8 +236,16 @@
     lax.fori_loop(0, 8, greet_lag, 0)
     pl.semaphore_wait(barrier, 31 + 3 + 8)
 
-    def peer(i):
-        return (c + i) % CTX
+    def each_peer(action, cores=(0, 2)):
+        def of_core(step, carry):
+            core = lax.rem(c + step, 2)
+            for dz, dy in STEPS:
+                action(lax.rem(z + dz, 4) * 8 + lax.rem(y + dy, 4) * 2 + core)
+            return carry
+
+        lax.fori_loop(*cores, of_core, 0)
+        if cores[1] == 2:
+            action(c + 1 - 2 * lax.rem(c, 2))
 
     def wait_bytes(ref, sem):
         pltpu.make_async_copy(ref, ref, sem).wait()
@@ -247,21 +257,18 @@
 
     loads["filt"].wait()
 
-    def send_filter(i, carry):
-        t = peer(i)
+    def send_filter(t):
         pltpu.make_async_remote_copy(
             src_ref=filt_cols(channel_block(t)), dst_ref=got_k.at[c, quarter],
             send_sem=ksend, recv_sem=krecv, device_id=(d, t), device_id_type=MESH,
         ).start()
-        return carry
-
-    lax.fori_loop(1, CTX, send_filter, 0)
+
+    each_peer(send_filter)
     own_copy = pltpu.make_async_copy(filt_cols(mine), got_k.at[c, quarter], own_sem)
     own_copy.start()
 
     def product_out(left, right, store, target, ssem, rsem):
-        def block(i, carry):
-            t = peer(i)
+        def block(t):
             b = channel_block(t)
             cols = pl.ds(pl.multiple_of(b * LANES, LANES), LANES)
             store[b] = left[:, cols].astype(F32) * right[:, cols].astype(F32)
@@ -269,9 +276,8 @@
                 src_ref=store.at[b], dst_ref=target.at[c],
                 send_sem=ssem, recv_sem=rsem, device_id=(d, t), device_id_type=MESH,
             ).start()
-            return carry
-
-        lax.fori_loop(1, CTX, block, 0)
+
+        each_peer(block)
         cols = pl.ds(pl.multiple_of(mine * LANES, LANES), LANES)
         target[c] = left[:, cols].astype(F32) * right[:, cols].astype(F32)
 
@@ -338,16 +344,16 @@
 
         lax.fori_loop(0, ROWS // 8, lead, 0)
 
-    def send_back(source, target, ssem, rsem):
-        def block(i, carry):
-            t = peer(i)
+    def send_back(source, target, ssem, rsem, cores=(0, 2)):
+        def block(t):
             pltpu.make_async_remote_copy(
                 src_ref=source.at[t], dst_ref=target.at[mine],
                 send_sem=ssem, recv_sem=rsem, device_id=(d, t), device_id_type=MESH,
             ).start()
-            return carry
-
-        lax.fori_loop(1, CTX, block, 0)
+
+        each_peer(block, cores)
+        if cores[1] != 2:
+            return None
         copy = pltpu.make_async_copy(source.at[c], target.at[mine], own_sem)
         copy.start()
         return copy
@@ -383,7 +389,7 @@
 
     inverse(spec_k, spec_g, True, send_b)
     conv_own.wait()
-    back_own = send_back(send_b, got_back, bsend, brecv)
+    send_back(send_b, got_back, bsend, brecv, (0, 1))
 
     wait_bytes(got_conv.at[blocks], crecv)
 
@@ -393,14 +399,8 @@
         return carry
 
     lax.fori_loop(0, CTX, finish_conv, 0)
-    outs = []
-
-    def write_out(index, source, target):
-        copy = pltpu.make_async_copy(source, target, out_sem.at[index])
-        copy.start()
-        outs.append(copy)
-
-    write_out(0, q_in, qg_hbm.at[0])
+    query_out = pltpu.make_async_copy(q_in, qg_hbm, out_sem.at[0])
+    query_out.start()
 
     for copy in share:
         copy.wait()
@@ -415,6 +415,7 @@
         return carry
 
     lax.fori_loop(0, 8, add_up, 0)
+    back_own = send_back(send_b, got_back, bsend, brecv, (1, 2))
     wait_bytes(lag, lrecv)
 
     def measure(i, carry):
@@ -443,67 +444,114 @@
         copy.wait()
     tile_row[...] = (tile_mine[...] + tile_x[0]) + (tile_x[1] + tile_x[2])
 
-    def spread(i, carry):
+    def spread(t):
         pltpu.make_async_remote_copy(
             src_ref=tile_row, dst_ref=tile_all.at[c],
-            send_sem=asend, recv_sem=arecv, device_id=(d, peer(i)), device_id_type=MESH,
+            send_sem=asend, recv_sem=arecv, device_id=(d, t), device_id_type=MESH,
         ).start()
-        return carry
-
-    lax.fori_loop(1, CTX, spread, 0)
+
+    each_peer(spread)
     tile_all[c] = tile_row[...]
 
+    lag_out = pltpu.make_async_copy(lag, lag_hbm, out_sem.at[1])
+    lag_out.start()
+    wait_bytes(tile_all.at[blocks], arecv)
+    total_ref[...] = jnp.sum(tile_all[...], axis=0)
     back_own.wait()
     wait_bytes(got_back.at[blocks], brecv)
-
-    def finish_back(b, carry):
-        cols = pl.ds(pl.multiple_of(b * LANES, LANES), LANES)
-        back = got_back[b]
-        keys, values = k_in[:, cols].astype(F32), v_in[:, cols].astype(F32)
-        v_in[:, cols] = (back * values).astype(BF16)
-        k_in[:, cols] = (back * keys).astype(BF16)
-        return carry
-
-    lax.fori_loop(0, CTX, finish_back, 0)
-    write_out(1, v_in, kg_hbm.at[0])
-    write_out(2, k_in, vg_hbm.at[0])
-
-    wait_bytes(tile_all.at[blocks], arecv)
-    everything = jnp.sum(tile_all[...], axis=0)
-    total_sq = jnp.sum(everything[:8])
-    bad_count = jnp.sum(everything[8:])
-    mean_sq = jnp.full((8, LANES), total_sq) * (1.0 / (PERIOD * 4096)) + 1e-06
-    factor = jnp.minimum(1.0, 1.0 / jnp.sqrt(mean_sq))[:1]
-    commit = (jnp.full((8, LANES), bad_count) == 0.0)[:1]
-    loads["own"].wait()
-    loads["m1"].wait()
-    loads["m2"].wait()
-
-    def step(h, carry):
-        cols = pl.ds(pl.multiple_of(h * LANES, LANES), LANES)
-        clipped = lag[h] * factor
-        first, second, weight = m1[:, cols], m2[:, cols], filt_own[:, cols]
-        first_next = beta_first * first + (1.0 - beta_first) * clipped
-        second_next = beta_second * second + (1.0 - beta_second) * clipped * clipped
-        update = (
-            first_next / correct_first / (jnp.sqrt(second_next / correct_second) + adam_epsilon)
-            + decay_rate * weight
-        )
-        filt_own[:, cols] = jnp.where(commit, weight - learn_rate * update, weight)
-        m1[:, cols] = jnp.where(commit, first_next, first)
-        m2[:, cols] = jnp.where(commit, second_next, second)
-        return carry
-
-    lax.fori_loop(0, 8, step, 0)
-    write_out(3, filt_own, nf_hbm)
-    write_out(4, m1, n1_hbm)
-    write_out(5, m2, n2_hbm)
 
     wait_bytes(got_k.at[blocks, quarter], ksend)
     wait_bytes(send_m.at[blocks], csend)
     wait_bytes(send_b.at[blocks], bsend)
     wait_bytes(summed, lsend)
     wait_bytes(tile_all.at[blocks], asend)
+    query_out.wait()
+    lag_out.wait()
+
+
+def finish(
+    qg_hbm, back_hbm, lag_hbm, total_ref, k_hbm, v_hbm, filt_hbm, m1_hbm, m2_hbm,
+    query_hbm, key_hbm, value_hbm, nf_hbm, n1_hbm, n2_hbm,
+    back, keys, values, query, lag, weight, first, second, in_sem, out_sem,
+):
+    d = lax.axis_index("dp")
+    parts = keys.shape[0]
+    width = keys.shape[2]
+    per = back.shape[0] // parts
+
+    def load(source, target, index):
+        copy = pltpu.make_async_copy(source, target, in_sem.at[index])
+        copy.start()
+        return copy
+
+    loads = []
+    for part in range(parts):
+        some, cols = pl.ds(part * per, per), pl.ds(part * width, width)
+        loads.append((
+            load(back_hbm.at[some], back.at[some], 3 * part),
+            load(k_hbm.at[0, :, cols], keys.at[part], 3 * part + 1),
+            load(v_hbm.at[0, :, cols], values.at[part], 3 * part + 2),
+        ))
+    state = [
+        load(lag_hbm, lag, 3 * parts),
+        load(filt_hbm.at[:, pl.ds(pl.multiple_of(d * 1024, 1024), 1024)], weight, 3 * parts + 1),
+        load(m1_hbm, first, 3 * parts + 2),
+        load(m2_hbm, second, 3 * parts + 3),
+    ]
+    query_in = load(qg_hbm, query, 3 * parts + 4)
+    outs = []
+
+    def store(source, target, index):
+        copy = pltpu.make_async_copy(source, target, out_sem.at[index])
+        copy.start()
+        outs.append(copy)
+
+    for part in range(parts):
+        for copy in loads[part]:
+            copy.wait()
+
+        def gradients(i, carry):
+            cols = pl.ds(pl.multiple_of(i * LANES, LANES), LANES)
+            value = back[part * per + i]
+            key_part = keys[part, :, cols].astype(F32)
+            keys[part, :, cols] = (value * values[part, :, cols].astype(F32)).astype(BF16)
+            values[part, :, cols] = (value * key_part).astype(BF16)
+            return carry
+
+        lax.fori_loop(0, per, gradients, 0)
+        cols = pl.ds(part * width, width)
+        store(keys.at[part], key_hbm.at[0, :, cols], 2 * part + 1)
+        store(values.at[part], value_hbm.at[0, :, cols], 2 * part + 2)
+
+    query_in.wait()
+    store(query, query_hbm.at[0], 0)
+    for copy in state:
+        copy.wait()
+    total_sq = jnp.sum(total_ref[:8])
+    bad_count = jnp.sum(total_ref[8:])
+    mean_sq = jnp.full((8, LANES), total_sq) * (1.0 / (PERIOD * 4096)) + 1e-06
+    factor = jnp.minimum(1.0, 1.0 / jnp.sqrt(mean_sq))[:1]
+    commit = (jnp.full((8, LANES), bad_count) == 0.0)[:1]
+
+    def step(h, carry):
+        cols = pl.ds(pl.multiple_of(h * LANES, LANES), LANES)
+        clipped = lag[h] * factor
+        m1, m2, filt = first[:, cols], second[:, cols], weight[:, cols]
+        first_next = beta_first * m1 + (1.0 - beta_first) * clipped
+        second_next = beta_second * m2 + (1.0 - beta_second) * clipped * clipped
+        update = (
+            first_next / correct_first / (jnp.sqrt(second_next / correct_second) + adam_epsilon)
+            + decay_rate * filt
+        )
+        weight[:, cols] = jnp.where(commit, filt - learn_rate * update, filt)
+        first[:, cols] = jnp.where(commit, first_next, m1)
+        second[:, cols] = jnp.where(commit, second_next, m2)
+        return carry
+
+    lax.fori_loop(0, 8, step, 0)
+    store(weight, nf_hbm, 2 * parts + 1)
+    store(first, n1_hbm, 2 * parts + 2)
+    store(second, n2_hbm, 2 * parts + 3)
     for copy in outs:
         copy.wait()
 
@@ -514,34 +562,53 @@
     wide = (CTX, ROWS, 2 * LANES)
     vmem = pltpu.VMEM
     dma = pltpu.SemaphoreType.DMA
-    anywhere = pl.BlockSpec(memory_space=pl.ANY)
+    anywhere = pl.BlockSpec(memory_space=pltpu.HBM)
+    either = pl.BlockSpec(memory_space=pl.ANY)
     stream = jax.ShapeDtypeStruct(query_act.shape, BF16)
     state = jax.ShapeDtypeStruct(first_moment.shape, F32)
-    return pl.pallas_call(
+    query_grad, back_in, lag_grad, total = pl.pallas_call(
         body,
-        out_shape=(stream, stream, stream, state, state, state),
-        in_specs=[anywhere] * 8,
-        out_specs=(anywhere,) * 6,
+        out_shape=(
+            jax.ShapeDtypeStruct((ROWS, 4096), BF16),
+            jax.ShapeDtypeStruct(block, F32),
+            jax.ShapeDtypeStruct((8, ROWS, LANES), F32),
+            jax.ShapeDtypeStruct((16, LANES), F32),
+        ),
+        in_specs=[anywhere] * 6,
+        out_specs=(either, either, either, pl.BlockSpec(memory_space=pltpu.VMEM)),
         scratch_shapes=[
             vmem((ROWS, 4096), BF16), vmem((ROWS, 4096), BF16),
             vmem((ROWS, 4096), BF16), vmem((ROWS, 4096), BF16),
-            vmem((32, 4096), F32), vmem((ROWS, 1024), F32),
-            vmem((ROWS, 1024), F32), vmem((ROWS, 1024), F32),
+            vmem((32, 4096), F32),
             vmem((4,) + wide, BF16),
             vmem(block, F32), vmem(block, F32), vmem(block, F32),
             vmem(block, F32), vmem(block, F32), vmem(block, F32),
             vmem(wide, F32), vmem(wide, F32), vmem(wide, F32), vmem(wide, F32),
-            vmem(block, F32), vmem(block, F32),
+            vmem(block, F32),
             vmem((3, 8, ROWS, LANES), F32), vmem((8, ROWS, LANES), F32), vmem((8, ROWS, LANES), F32),
             vmem((16, LANES), F32), vmem((3, 16, LANES), F32), vmem((16, LANES), F32),
             vmem((CTX, 16, LANES), F32),
-            dma((9,)), dma((6,)), dma, dma, dma((3,)), dma((3,)), dma, dma, dma, dma,
+            dma((6,)), dma((2,)), dma, dma, dma((3,)), dma((3,)), dma, dma, dma, dma,
             dma, dma, dma, dma, dma((3, 4)), dma((3, 4)), dma, dma, dma((3,)), dma((3,)), dma, dma, dma,
         ],
         compiler_params=pltpu.CompilerParams(
-            collective_id=0, has_side_effects=True, vmem_limit_bytes=60 * 2**20
+            collective_id=0, has_side_effects=True, vmem_limit_bytes=VMEM_MIB * 2**20
         ),
-    )(query_act, key_act, value_act, out_grad, filter_weight, first_moment, second_moment, table)
+    )(query_act, key_act, value_act, out_grad, filter_weight, table)
+    cuts = 4
+    return pl.pallas_call(
+        finish,
+        out_shape=(stream, stream, stream, state, state, state),
+        in_specs=[either] * 3 + [pl.BlockSpec(memory_space=pltpu.VMEM)] + [anywhere] * 5,
+        out_specs=(anywhere,) * 6,
+        scratch_shapes=[
+            vmem(block, F32), vmem((cuts, ROWS, 4096 // cuts), BF16), vmem((cuts, ROWS, 4096 // cuts), BF16),
+            vmem((ROWS, 4096), BF16),
+            vmem((8, ROWS, LANES), F32), vmem((ROWS, 1024), F32), vmem((ROWS, 1024), F32), vmem((ROWS, 1024), F32),
+            dma((3 * cuts + 5,)), dma((2 * cuts + 4,)),
+        ],
+        compiler_params=pltpu.CompilerParams(vmem_limit_bytes=VMEM_MIB * 2**20),
+    )(query_grad, back_in, lag_grad, total, key_act, value_act, filter_weight, first_moment, second_moment)
 
 
 def solution(mesh):

time: 166 us -> 144 us (0.87)
  local copies, waits for them, and re-layouts: 11.5 us -> 0 us
  Pallas kernels: 153 us -> 143 us
    unnamed x8 -> x0, local copies, waits for them, and re-layouts: 11.5 us -> none
    pallas_call x1 -> x2, Pallas kernels: 153 us -> 143 us  [the longest x1 136 us: on_device(): pl.pallas_call(body, out_shape=(jax.ShapeDtypeStruct((ROWS, 4096), BF16),...]
where the time goes in v2:
time: 144 us
  Pallas kernels  143 us (99%)
    pallas_call x1, Pallas kernels, on_device(): pl.pallas_call(body, out_shape=(jax.ShapeDtypeStruct((ROWS, 4096), BF16),...  136 us
    pallas_call x1, Pallas kernels, on_device(): pl.pallas_call(finish, out_shape=(stream, stream, stream, state, state, s...  6.8 us

profile of v2, /device:TPU:1, one launch (start us, length us, event | category | flops | bytes accessed | tf_op | source)
XLA Modules:
  0.0 143.8 jit_solution(4935884446023765658)
XLA Ops:
  0.6 136.4 %shard_map.127 = (bf16[128,4096]{1,0:T(8,128)(2,1)}, f32[32,128,128]{2,1,0:T(8,128)}, f32[8,128,128]{2,1,0:T(8,128)}, f32[16,128]{1,0:T(8,128)}) custom-call(bf16[1,128,4096]{2,1,0:T(8,128)(2,1)} %q_hbm.1, bf16[1,128,4096]{2,1,0:T(8,128)(2,1)} %k_hbm.3, bf16[1,128,4096]{2,1,0:T(8,128)(2,1)} %v_hbm.3, bf16[1,128,4096]{2,1,0:T(8,128)(2,1)} %g_hbm.1, ...), custom_call_target="tpu_custom_call" | custom-call | tf_op jit(solution)/shard_map/pallas_call | solution.py:569
  137.0 6.8 %shard_map.128 = (bf16[1,128,4096]{2,1,0:T(8,128)(2,1)}, bf16[1,128,4096]{2,1,0:T(8,128)(2,1)}, bf16[1,128,4096]{2,1,0:T(8,128)(2,1)}, f32[128,1024]{1,0:T(8,128...) custom-call(bf16[128,4096]{1,0:T(8,128)(2,1)} %get-tuple-element.10.qg_hbm, f32[32,128,128]{2,1,0:T(8,128)} %get-tuple-element.11.back_hbm, ...), custom_call_target="tpu_custom_call" | custom-call | tf_op jit(solution)/shard_map/pallas_call | solution.py:599

commit v3 on v2

--- a/solution.py
+++ b/solution.py
@@ -17,7 +17,8 @@
 CTX = 32
 ROWS = 128
 LANES = 128
-VMEM_MIB = 60
+VMEM_MIB = 51
+BACK_EARLY = 7
 PERIOD = CTX * ROWS
 STEPS = (
     (2, 2), (2, 3), (3, 2), (2, 1), (1, 2), (2, 0), (0, 2), (1, 1),
@@ -179,7 +180,7 @@
 
 def body(
     q_hbm, k_hbm, v_hbm, g_hbm, filt_hbm, tab_hbm,
-    qg_hbm, got_back, lag_hbm, total_ref,
+    qg_hbm, got_back, lag_hbm, own_hbm, total_ref,
     q_in, k_in, v_in, g_in, filt_part, tab,
     send_m, send_g, send_b, got_m, got_k, got_g, work, spec_k, spec_m, spec_g,
     got_conv, parts, summed, lag,
@@ -205,6 +206,7 @@
     load("g", 3, g_hbm.at[0], g_in)
     load("q", 4, q_hbm.at[0], q_in)
     load("tab", 5, tab_hbm, tab)
+    load("own", 6, filt_hbm.at[:, pl.ds(pl.multiple_of(d * 1024, 1024), 1024)], own_hbm)
 
     level = (z + y) % 4
     helper = 2 * (1 - level % 2) + level // 2
@@ -236,16 +238,21 @@
     lax.fori_loop(0, 8, greet_lag, 0)
     pl.semaphore_wait(barrier, 31 + 3 + 8)
 
-    def each_peer(action, cores=(0, 2)):
+    def some_peers(action, step, first, last):
+        core = lax.rem(c + step, 2)
+        for dz, dy in STEPS[first:last]:
+            action(lax.rem(z + dz, 4) * 8 + lax.rem(y + dy, 4) * 2 + core)
+
+    def sibling(action):
+        action(c + 1 - 2 * lax.rem(c, 2))
+
+    def each_peer(action):
         def of_core(step, carry):
-            core = lax.rem(c + step, 2)
-            for dz, dy in STEPS:
-                action(lax.rem(z + dz, 4) * 8 + lax.rem(y + dy, 4) * 2 + core)
+            some_peers(action, step, 0, len(STEPS))
             return carry
 
-        lax.fori_loop(*cores, of_core, 0)
-        if cores[1] == 2:
-            action(c + 1 - 2 * lax.rem(c, 2))
+        lax.fori_loop(0, 2, of_core, 0)
+        sibling(action)
 
     def wait_bytes(ref, sem):
         pltpu.make_async_copy(ref, ref, sem).wait()
@@ -267,23 +274,38 @@
     own_copy = pltpu.make_async_copy(filt_cols(mine), got_k.at[c, quarter], own_sem)
     own_copy.start()
 
-    def product_out(left, right, store, target, ssem, rsem):
-        def block(t):
-            b = channel_block(t)
-            cols = pl.ds(pl.multiple_of(b * LANES, LANES), LANES)
-            store[b] = left[:, cols].astype(F32) * right[:, cols].astype(F32)
-            pltpu.make_async_remote_copy(
-                src_ref=store.at[b], dst_ref=target.at[c],
-                send_sem=ssem, recv_sem=rsem, device_id=(d, t), device_id_type=MESH,
-            ).start()
-
-        each_peer(block)
-        cols = pl.ds(pl.multiple_of(mine * LANES, LANES), LANES)
-        target[c] = left[:, cols].astype(F32) * right[:, cols].astype(F32)
+    def product(left, right, b):
+        cols = pl.ds(pl.multiple_of(b * LANES, LANES), LANES)
+        return left[:, cols].astype(F32) * right[:, cols].astype(F32)
+
+    def send_block(t, store, target, ssem, rsem):
+        pltpu.make_async_remote_copy(
+            src_ref=store.at[channel_block(t)], dst_ref=target.at[c],
+            send_sem=ssem, recv_sem=rsem, device_id=(d, t), device_id_type=MESH,
+        ).start()
 
     loads["k"].wait()
     loads["v"].wait()
-    product_out(k_in, v_in, send_m, got_m, msend, mrecv)
+
+    def mixed(b, carry):
+        send_m[b] = product(k_in, v_in, b)
+        return carry
+
+    lax.fori_loop(0, CTX, mixed, 0)
+    got_m[c] = send_m[mine]
+
+    blocks = pl.ds(0, CTX - 1)
+    each_peer(lambda t: send_block(t, send_m, got_m, msend, mrecv))
+
+    loads["g"].wait()
+    loads["q"].wait()
+
+    def gated(b, carry):
+        send_g[b] = product(g_in, q_in, b)
+        return carry
+
+    lax.fori_loop(0, CTX, gated, 0)
+    got_g[c] = send_g[mine]
 
     own_copy.wait()
     wait_bytes(got_k.at[pl.ds(0, 31), quarter], krecv)
@@ -297,9 +319,8 @@
         copy.start()
         share.append(copy)
 
-    loads["g"].wait()
-    loads["q"].wait()
-    product_out(g_in, q_in, send_g, got_g, gsend, grecv)
+    wait_bytes(send_m.at[blocks], msend)
+    each_peer(lambda t: send_block(t, send_g, got_g, gsend, grecv))
 
     def forward(got, spec, scale=None):
         def lead(i, carry):
@@ -344,34 +365,33 @@
 
         lax.fori_loop(0, ROWS // 8, lead, 0)
 
-    def send_back(source, target, ssem, rsem, cores=(0, 2)):
-        def block(t):
+    def result_block(source, target, ssem, rsem):
+        def send(t):
             pltpu.make_async_remote_copy(
                 src_ref=source.at[t], dst_ref=target.at[mine],
                 send_sem=ssem, recv_sem=rsem, device_id=(d, t), device_id_type=MESH,
             ).start()
 
-        each_peer(block, cores)
-        if cores[1] != 2:
-            return None
+        return send
+
+    def keep_own(source, target):
         copy = pltpu.make_async_copy(source.at[c], target.at[mine], own_sem)
         copy.start()
         return copy
 
-    blocks = pl.ds(0, CTX - 1)
     loads["tab"].wait()
     wait_bytes(got_m.at[blocks], mrecv)
     forward(got_m, spec_m)
     for copy in share:
         copy.wait()
     forward(got_k, spec_k, PERIOD**-0.5)
-    wait_bytes(send_m.at[blocks], msend)
     inverse(spec_k, spec_m, False, send_m)
-    conv_own = send_back(send_m, got_conv, csend, crecv)
+    wait_bytes(send_g.at[blocks], gsend)
+    each_peer(result_block(send_m, got_conv, csend, crecv))
+    conv_own = keep_own(send_m, got_conv)
 
     wait_bytes(got_g.at[blocks], grecv)
     forward(got_g, spec_g)
-    wait_bytes(send_g.at[blocks], gsend)
     inverse(spec_m, spec_g, True, send_g)
 
     share = []
@@ -389,7 +409,9 @@
 
     inverse(spec_k, spec_g, True, send_b)
     conv_own.wait()
-    send_back(send_b, got_back, bsend, brecv, (0, 1))
+    wait_bytes(send_m.at[blocks], csend)
+    back_block = result_block(send_b, got_back, bsend, brecv)
+    some_peers(back_block, 0, 0, 15)
 
     wait_bytes(got_conv.at[blocks], crecv)
 
@@ -406,21 +428,10 @@
         copy.wait()
 
     def add_up(i, carry):
-        t = lag_target(i, d)
-        summed[i] = (send_g[t] + parts[0, i]) + (parts[1, i] + parts[2, i])
-        pltpu.make_async_remote_copy(
-            src_ref=summed.at[i], dst_ref=lag.at[slot],
-            send_sem=lsend, recv_sem=lrecv, device_id=(plane, t), device_id_type=MESH,
-        ).start()
-        return carry
-
-    lax.fori_loop(0, 8, add_up, 0)
-    back_own = send_back(send_b, got_back, bsend, brecv, (1, 2))
-    wait_bytes(lag, lrecv)
-
-    def measure(i, carry):
         squares, bad = carry
-        value = lag[i].reshape(16, 8, LANES)
+        value = (send_g[lag_target(i, d)] + parts[0, i]) + (parts[1, i] + parts[2, i])
+        summed[i] = value
+        value = value.reshape(16, 8, LANES)
         finite = jnp.abs(value) < jnp.inf
         return (
             squares + jnp.sum(value * value, axis=0),
@@ -428,7 +439,7 @@
         )
 
     nothing = jnp.zeros((8, LANES), F32)
-    squares, bad = lax.fori_loop(0, 8, measure, (nothing, nothing))
+    squares, bad = lax.fori_loop(0, 8, add_up, (nothing, nothing))
     tile_mine[:8] = squares
     tile_mine[8:] = bad
     share = []
@@ -440,6 +451,16 @@
         )
         copy.start()
         share.append(copy)
+
+    def send_lag(i, carry):
+        pltpu.make_async_remote_copy(
+            src_ref=summed.at[i], dst_ref=lag.at[slot],
+            send_sem=lsend, recv_sem=lrecv, device_id=(plane, lag_target(i, d)), device_id_type=MESH,
+        ).start()
+        return carry
+
+    lax.fori_loop(0, 8, send_lag, 0)
+    some_peers(back_block, 1, 0, BACK_EARLY)
     for copy in share:
         copy.wait()
     tile_row[...] = (tile_mine[...] + tile_x[0]) + (tile_x[1] + tile_x[2])
@@ -452,6 +473,10 @@
 
     each_peer(spread)
     tile_all[c] = tile_row[...]
+    some_peers(back_block, 1, BACK_EARLY, 15)
+    sibling(back_block)
+    back_own = keep_own(send_b, got_back)
+    wait_bytes(lag, lrecv)
 
     lag_out = pltpu.make_async_copy(lag, lag_hbm, out_sem.at[1])
     lag_out.start()
@@ -461,44 +486,22 @@
     wait_bytes(got_back.at[blocks], brecv)
 
     wait_bytes(got_k.at[blocks, quarter], ksend)
-    wait_bytes(send_m.at[blocks], csend)
     wait_bytes(send_b.at[blocks], bsend)
     wait_bytes(summed, lsend)
     wait_bytes(tile_all.at[blocks], asend)
     query_out.wait()
     lag_out.wait()
+    loads["own"].wait()
 
 
 def finish(
-    qg_hbm, back_hbm, lag_hbm, total_ref, k_hbm, v_hbm, filt_hbm, m1_hbm, m2_hbm,
+    query_ref, back_ref, lag_ref, total_ref, k_ref, v_ref, filt_ref, m1_ref, m2_ref,
     query_hbm, key_hbm, value_hbm, nf_hbm, n1_hbm, n2_hbm,
-    back, keys, values, query, lag, weight, first, second, in_sem, out_sem,
+    keys, values, weight, first, second, out_sem,
 ):
-    d = lax.axis_index("dp")
     parts = keys.shape[0]
     width = keys.shape[2]
-    per = back.shape[0] // parts
-
-    def load(source, target, index):
-        copy = pltpu.make_async_copy(source, target, in_sem.at[index])
-        copy.start()
-        return copy
-
-    loads = []
-    for part in range(parts):
-        some, cols = pl.ds(part * per, per), pl.ds(part * width, width)
-        loads.append((
-            load(back_hbm.at[some], back.at[some], 3 * part),
-            load(k_hbm.at[0, :, cols], keys.at[part], 3 * part + 1),
-            load(v_hbm.at[0, :, cols], values.at[part], 3 * part + 2),
-        ))
-    state = [
-        load(lag_hbm, lag, 3 * parts),
-        load(filt_hbm.at[:, pl.ds(pl.multiple_of(d * 1024, 1024), 1024)], weight, 3 * parts + 1),
-        load(m1_hbm, first, 3 * parts + 2),
-        load(m2_hbm, second, 3 * parts + 3),
-    ]
-    query_in = load(qg_hbm, query, 3 * parts + 4)
+    per = width // LANES
     outs = []
 
     def store(source, target, index):
@@ -506,16 +509,15 @@
         copy.start()
         outs.append(copy)
 
+    store(query_ref, query_hbm.at[0], 0)
     for part in range(parts):
-        for copy in loads[part]:
-            copy.wait()
 
         def gradients(i, carry):
             cols = pl.ds(pl.multiple_of(i * LANES, LANES), LANES)
-            value = back[part * per + i]
-            key_part = keys[part, :, cols].astype(F32)
-            keys[part, :, cols] = (value * values[part, :, cols].astype(F32)).astype(BF16)
-            values[part, :, cols] = (value * key_part).astype(BF16)
+            wide_cols = pl.ds(pl.multiple_of(part * width + i * LANES, LANES), LANES)
+            value = back_ref[part * per + i]
+            keys[part, :, cols] = (value * v_ref[0, :, wide_cols].astype(F32)).astype(BF16)
+            values[part, :, cols] = (value * k_ref[0, :, wide_cols].astype(F32)).astype(BF16)
             return carry
 
         lax.fori_loop(0, per, gradients, 0)
@@ -523,10 +525,6 @@
         store(keys.at[part], key_hbm.at[0, :, cols], 2 * part + 1)
         store(values.at[part], value_hbm.at[0, :, cols], 2 * part + 2)
 
-    query_in.wait()
-    store(query, query_hbm.at[0], 0)
-    for copy in state:
-        copy.wait()
     total_sq = jnp.sum(total_ref[:8])
     bad_count = jnp.sum(total_ref[8:])
     mean_sq = jnp.full((8, LANES), total_sq) * (1.0 / (PERIOD * 4096)) + 1e-06
@@ -535,8 +533,8 @@
 
     def step(h, carry):
         cols = pl.ds(pl.multiple_of(h * LANES, LANES), LANES)
-        clipped = lag[h] * factor
-        m1, m2, filt = first[:, cols], second[:, cols], weight[:, cols]
+        clipped = lag_ref[h] * factor
+        m1, m2, filt = m1_ref[:, cols], m2_ref[:, cols], filt_ref[:, cols]
         first_next = beta_first * m1 + (1.0 - beta_first) * clipped
         second_next = beta_second * m2 + (1.0 - beta_second) * clipped * clipped
         update = (
@@ -566,16 +564,17 @@
     either = pl.BlockSpec(memory_space=pl.ANY)
     stream = jax.ShapeDtypeStruct(query_act.shape, BF16)
     state = jax.ShapeDtypeStruct(first_moment.shape, F32)
-    query_grad, back_in, lag_grad, total = pl.pallas_call(
+    query_grad, back_in, lag_grad, own_filter, total = pl.pallas_call(
         body,
         out_shape=(
             jax.ShapeDtypeStruct((ROWS, 4096), BF16),
             jax.ShapeDtypeStruct(block, F32),
             jax.ShapeDtypeStruct((8, ROWS, LANES), F32),
+            state,
             jax.ShapeDtypeStruct((16, LANES), F32),
         ),
         in_specs=[anywhere] * 6,
-        out_specs=(either, either, either, pl.BlockSpec(memory_space=pltpu.VMEM)),
+        out_specs=(either, either, either, either, pl.BlockSpec(memory_space=pltpu.VMEM)),
         scratch_shapes=[
             vmem((ROWS, 4096), BF16), vmem((ROWS, 4096), BF16),
             vmem((ROWS, 4096), BF16), vmem((ROWS, 4096), BF16),
@@ -588,7 +587,7 @@
             vmem((3, 8, ROWS, LANES), F32), vmem((8, ROWS, LANES), F32), vmem((8, ROWS, LANES), F32),
             vmem((16, LANES), F32), vmem((3, 16, LANES), F32), vmem((16, LANES), F32),
             vmem((CTX, 16, LANES), F32),
-            dma((6,)), dma((2,)), dma, dma, dma((3,)), dma((3,)), dma, dma, dma, dma,
+            dma((7,)), dma((2,)), dma, dma, dma((3,)), dma((3,)), dma, dma, dma, dma,
             dma, dma, dma, dma, dma((3, 4)), dma((3, 4)), dma, dma, dma((3,)), dma((3,)), dma, dma, dma,
         ],
         compiler_params=pltpu.CompilerParams(
@@ -596,19 +595,19 @@
         ),
     )(query_act, key_act, value_act, out_grad, filter_weight, table)
     cuts = 4
+    local = pl.BlockSpec(memory_space=pltpu.VMEM)
     return pl.pallas_call(
         finish,
         out_shape=(stream, stream, stream, state, state, state),
-        in_specs=[either] * 3 + [pl.BlockSpec(memory_space=pltpu.VMEM)] + [anywhere] * 5,
+        in_specs=[local] * 9,
         out_specs=(anywhere,) * 6,
         scratch_shapes=[
-            vmem(block, F32), vmem((cuts, ROWS, 4096 // cuts), BF16), vmem((cuts, ROWS, 4096 // cuts), BF16),
-            vmem((ROWS, 4096), BF16),
-            vmem((8, ROWS, LANES), F32), vmem((ROWS, 1024), F32), vmem((ROWS, 1024), F32), vmem((ROWS, 1024), F32),
-            dma((3 * cuts + 5,)), dma((2 * cuts + 4,)),
+            vmem((cuts, ROWS, 4096 // cuts), BF16), vmem((cuts, ROWS, 4096 // cuts), BF16),
+            vmem((ROWS, 1024), F32), vmem((ROWS, 1024), F32), vmem((ROWS, 1024), F32),
+            dma((2 * cuts + 4,)),
         ],
-        compiler_params=pltpu.CompilerParams(vmem_limit_bytes=VMEM_MIB * 2**20),
-    )(query_grad, back_in, lag_grad, total, key_act, value_act, filter_weight, first_moment, second_moment)
+        compiler_params=pltpu.CompilerParams(vmem_limit_bytes=16 * 2**20),
+    )(query_grad, back_in, lag_grad, total, key_act, value_act, own_filter, first_moment, second_moment)
 
 
 def solution(mesh):

time: 144 us -> 138 us (0.958)
  Pallas kernels: 143 us -> 136 us
  local copies, waits for them, and re-layouts: 0 us -> 1.6 us
    pallas_call x1, Pallas kernels: 6.8 us -> 2.81 us  [on_device(): pl.pallas_call(finish, out_shape=(stream, stream, stream, state, state, s...]
    pallas_call x1, Pallas kernels: 136 us -> 133 us  [on_device(): pl.pallas_call(body, out_shape=(jax.ShapeDtypeStruct((ROWS, 4096), BF16),...]
    unnamed x0 -> x10, local copies, waits for them, and re-layouts: none -> 1.6 us
where the time goes in v3:
time: 138 us
  Pallas kernels  136 us (99%)
  local copies, waits for them, and re-layouts  1.6 us (1%)
    pallas_call x1, Pallas kernels, on_device(): pl.pallas_call(body, out_shape=(jax.ShapeDtypeStruct((ROWS, 4096), BF16),...  133 us
    pallas_call x1, Pallas kernels, on_device(): pl.pallas_call(finish, out_shape=(stream, stream, stream, state, state, s...  2.81 us

profile of v3, /device:TPU:1, one launch (start us, length us, event | category | flops | bytes accessed | tf_op | source)
XLA Modules:
  0.0 138.1 jit_solution(576447707675963559)
XLA Ops:
  0.6 0.0 copy-start.1
  0.6 0.0 copy-start
  0.7 0.0 copy-start.4
  0.7 0.0 copy-start.3
  0.7 133.0 %shard_map.127 = (bf16[128,4096]{1,0:T(8,128)(2,1)S(1)}, f32[32,128,128]{2,1,0:T(8,128)}, f32[8,128,128]{2,1,0:T(8,128)S(1)}, f32[128,1024]{1,0:T(8,128)S(1)}, f32[16,128]{1,0:T(8,128)S(1)}) custom-call(bf16[1,128,4096]{2,1,0:T(8,128)(2,1)} %q_hbm.1, bf16[1,128,4096]{2,1,0:T(8,128)(2,1)} %k_ref.1, bf16[1,128,4096]{2,1,0:T(8,128)(2,1)} %v_ref.1, ...), custom_call_target="tpu_custom_call" | custom-call | tf_op jit(solution)/shard_map/pallas_call | solution.py:567
  133.7 0.0 copy-done.1
  133.7 0.0 copy-done
  133.7 0.0 copy-done.4
  133.7 0.0 copy-done.3
  133.7 0.0 copy-start.2
  133.7 1.6 %copy-done.2 = f32[32,128,128]{2,1,0:T(8,128)S(1)} copy-done((f32[32,128,128]{2,1,0:T(8,128)S(1)}, f32[32,128,128]{2,1,0:T(8,128)}, u32[]{:S(2)}) %copy-start.2) | copy-done | bytes 2097176
  135.3 2.8 %shard_map.128 = (bf16[1,128,4096]{2,1,0:T(8,128)(2,1)}, bf16[1,128,4096]{2,1,0:T(8,128)(2,1)}, bf16[1,128,4096]{2,1,0:T(8,128)(2,1)}, f32[128,1024]{1,0:T(8,128...) custom-call(bf16[128,4096]{1,0:T(8,128)(2,1)S(1)} %get-tuple-element.11.query_ref, f32[32,128,128]{2,1,0:T(8,128)S(1)} %copy-done.2, ...), custom_call_target="tpu_custom_call" | custom-call | tf_op jit(solution)/shard_map/pallas_call | solution.py:599
Async XLA Ops:
  0.6 133.0 %copy-start.1 = (bf16[1,128,4096]{2,1,0:T(8,128)(2,1)S(1)}, bf16[1,128,4096]{2,1,0:T(8,128)(2,1)}, u32[]{:S(2)}) copy-start(bf16[1,128,4096]{2,1,0:T(8,128)(2,1)} %v_ref.1) | copy-start | bytes 3145732
  0.6 133.0 %copy-start = (bf16[1,128,4096]{2,1,0:T(8,128)(2,1)S(1)}, bf16[1,128,4096]{2,1,0:T(8,128)(2,1)}, u32[]{:S(2)}) copy-start(bf16[1,128,4096]{2,1,0:T(8,128)(2,1)} %k_ref.1) | copy-start | bytes 3145732
  0.7 133.0 %copy-start.4 = (f32[128,1024]{1,0:T(8,128)S(1)}, f32[128,1024]{1,0:T(8,128)}, u32[]{:S(2)}) copy-start(f32[128,1024]{1,0:T(8,128)} %m2_ref.1) | copy-start | bytes 1572868
  0.7 133.0 %copy-start.3 = (f32[128,1024]{1,0:T(8,128)S(1)}, f32[128,1024]{1,0:T(8,128)}, u32[]{:S(2)}) copy-start(f32[128,1024]{1,0:T(8,128)} %m1_ref.1) | copy-start | bytes 1572868
  133.7 1.6 %copy-start.2 = (f32[32,128,128]{2,1,0:T(8,128)S(1)}, f32[32,128,128]{2,1,0:T(8,128)}, u32[]{:S(2)}) copy-start(f32[32,128,128]{2,1,0:T(8,128)} %get-tuple-element.12.back_ref) | copy-start | bytes 6291460

commit v4 on v3

--- a/solution.py
+++ b/solution.py
@@ -203,10 +203,6 @@
     load("filt", 0, filt_hbm.at[pl.ds(pl.multiple_of(d * 32, 32), 32)], filt_part)
     load("k", 1, k_hbm.at[0], k_in)
     load("v", 2, v_hbm.at[0], v_in)
-    load("g", 3, g_hbm.at[0], g_in)
-    load("q", 4, q_hbm.at[0], q_in)
-    load("tab", 5, tab_hbm, tab)
-    load("own", 6, filt_hbm.at[:, pl.ds(pl.multiple_of(d * 1024, 1024), 1024)], own_hbm)
 
     level = (z + y) % 4
     helper = 2 * (1 - level % 2) + level // 2
@@ -286,6 +282,8 @@
 
     loads["k"].wait()
     loads["v"].wait()
+    load("g", 3, g_hbm.at[0], g_in)
+    load("q", 4, q_hbm.at[0], q_in)
 
     def mixed(b, carry):
         send_m[b] = product(k_in, v_in, b)
@@ -297,6 +295,9 @@
     blocks = pl.ds(0, CTX - 1)
     each_peer(lambda t: send_block(t, send_m, got_m, msend, mrecv))
 
+    load("tab", 5, tab_hbm, tab)
+    load("own", 6, filt_hbm.at[:, pl.ds(pl.multiple_of(d * 1024, 1024), 1024)], own_hbm)
+
     loads["g"].wait()
     loads["q"].wait()
 
@@ -310,7 +311,7 @@
     own_copy.wait()
     wait_bytes(got_k.at[pl.ds(0, 31), quarter], krecv)
     share = []
-    for step in range(1, DP):
+    for step in (1, 3, 2):
         copy = pltpu.make_async_remote_copy(
             src_ref=got_k.at[:, quarter], dst_ref=got_k.at[:, quarter],
             send_sem=kxsend.at[step - 1], recv_sem=kxrecv.at[step - 1],
@@ -395,7 +396,7 @@
     inverse(spec_m, spec_g, True, send_g)
 
     share = []
-    for step in range(1, DP):
+    for step in (1, 3, 2):
         to = (d + step) % DP
         for pair in range(4):
             copy = pltpu.make_async_remote_copy(

time: 138 us -> 136 us (0.986); the launches traced: 138 us -> 135 us
  Pallas kernels: 136 us -> 132 us
    pallas_call x1, Pallas kernels: 133 us -> 129 us  [on_device(): pl.pallas_call(body, out_shape=(jax.ShapeDtypeStruct((ROWS, 4096), BF16),...]
where the time goes in v4:
time: 136 us; the launch traced here: 135 us
  Pallas kernels  132 us (97%)
  local copies, waits for them, and re-layouts  1.6 us (1%)
    pallas_call x1, Pallas kernels, on_device(): pl.pallas_call(body, out_shape=(jax.ShapeDtypeStruct((ROWS, 4096), BF16),...  129 us
    pallas_call x1, Pallas kernels, on_device(): pl.pallas_call(finish, out_shape=(stream, stream, stream, state, state, s...  2.81 us

profile of v4, /device:TPU:1, one launch (start us, length us, event | category | flops | bytes accessed | tf_op | source)
XLA Modules:
  0.0 134.6 jit_solution(349783169386513108)
XLA Ops:
  0.6 0.0 copy-start.1
  0.6 0.0 copy-start
  0.7 0.0 copy-start.4
  0.7 0.0 copy-start.3
  0.7 129.5 %shard_map.127 = (bf16[128,4096]{1,0:T(8,128)(2,1)S(1)}, f32[32,128,128]{2,1,0:T(8,128)}, f32[8,128,128]{2,1,0:T(8,128)S(1)}, f32[128,1024]{1,0:T(8,128)S(1)}, f32[16,128]{1,0:T(8,128)S(1)}) custom-call(bf16[1,128,4096]{2,1,0:T(8,128)(2,1)} %q_hbm.1, bf16[1,128,4096]{2,1,0:T(8,128)(2,1)} %k_ref.1, bf16[1,128,4096]{2,1,0:T(8,128)(2,1)} %v_ref.1, ...), custom_call_target="tpu_custom_call" | custom-call | tf_op jit(solution)/shard_map/pallas_call | solution.py:568
  130.2 0.0 copy-done.1
  130.2 0.0 copy-done
  130.2 0.0 copy-done.4
  130.2 0.0 copy-done.3
  130.2 0.0 copy-start.2
  130.2 1.6 %copy-done.2 = f32[32,128,128]{2,1,0:T(8,128)S(1)} copy-done((f32[32,128,128]{2,1,0:T(8,128)S(1)}, f32[32,128,128]{2,1,0:T(8,128)}, u32[]{:S(2)}) %copy-start.2) | copy-done | bytes 2097176
  131.8 2.8 %shard_map.128 = (bf16[1,128,4096]{2,1,0:T(8,128)(2,1)}, bf16[1,128,4096]{2,1,0:T(8,128)(2,1)}, bf16[1,128,4096]{2,1,0:T(8,128)(2,1)}, f32[128,1024]{1,0:T(8,128...) custom-call(bf16[128,4096]{1,0:T(8,128)(2,1)S(1)} %get-tuple-element.11.query_ref, f32[32,128,128]{2,1,0:T(8,128)S(1)} %copy-done.2, ...), custom_call_target="tpu_custom_call" | custom-call | tf_op jit(solution)/shard_map/pallas_call | solution.py:600
Async XLA Ops:
  0.6 129.5 %copy-start.1 = (bf16[1,128,4096]{2,1,0:T(8,128)(2,1)S(1)}, bf16[1,128,4096]{2,1,0:T(8,128)(2,1)}, u32[]{:S(2)}) copy-start(bf16[1,128,4096]{2,1,0:T(8,128)(2,1)} %v_ref.1) | copy-start | bytes 3145732
  0.6 129.5 %copy-start = (bf16[1,128,4096]{2,1,0:T(8,128)(2,1)S(1)}, bf16[1,128,4096]{2,1,0:T(8,128)(2,1)}, u32[]{:S(2)}) copy-start(bf16[1,128,4096]{2,1,0:T(8,128)(2,1)} %k_ref.1) | copy-start | bytes 3145732
  0.7 129.5 %copy-start.4 = (f32[128,1024]{1,0:T(8,128)S(1)}, f32[128,1024]{1,0:T(8,128)}, u32[]{:S(2)}) copy-start(f32[128,1024]{1,0:T(8,128)} %m2_ref.1) | copy-start | bytes 1572868
  0.7 129.5 %copy-start.3 = (f32[128,1024]{1,0:T(8,128)S(1)}, f32[128,1024]{1,0:T(8,128)}, u32[]{:S(2)}) copy-start(f32[128,1024]{1,0:T(8,128)} %m1_ref.1) | copy-start | bytes 1572868
  130.2 1.6 %copy-start.2 = (f32[32,128,128]{2,1,0:T(8,128)S(1)}, f32[32,128,128]{2,1,0:T(8,128)}, u32[]{:S(2)}) copy-start(f32[32,128,128]{2,1,0:T(8,128)} %get-tuple-element.12.back_ref) | copy-start | bytes 6291460
